TPU v7x, 128 devices: a whole 4x4x4 slice. The times are simulated.
128 devices in a mesh: slide: 2 (over x_hi), sx: 16 (over y, x_lo, core), sy: 4 (over z).
Axes of the slice: x: 4 (x_hi: 2, x_lo: 2; x = x_hi * 2 + x_lo), y: 4, z: 4, core: 2. Of those that a mesh axis runs over, the one named last changes fastest.
Arguments:
- features: bfloat16 [1024, 128, 256], P(('slide', 'sx'), 'sy'), parts along dimension 0, may hold values from -6 to 6
- return_slot: int32 [128, 16], P(('slide', 'sx'), 'sy'), parts along dimension 0, may hold values from -1 to 31, as said below
- returned_grads: bfloat16 [4, 1024, 512], P('sy', ('slide', 'sx')), parts along dimension 1, may hold values from -6 to 6
- conv_weight: float32 [7, 7, 256], replicated, may hold values from -0.875 to 0.875
- conv_bias: float32 [256], replicated, may hold values from -3 to 3
- norm_gain: float32 [256], replicated, may hold values from 0.1 to 1.9
- norm_bias: float32 [256], replicated, may hold values from -3 to 3
- expand_weight: bfloat16 [256, 1024], replicated, may hold values from -0.375 to 0.375
- expand_bias: float32 [1024], replicated, may hold values from -3 to 3
- project_weight: bfloat16 [1024, 256], replicated, may hold values from -0.1875 to 0.1875
- project_bias: float32 [256], replicated, may hold values from -3 to 3
- layer_scale: float32 [256], replicated, may hold values from 0.5 to 1.5
- down_gain: float32 [256], replicated, may hold values from 0.1 to 1.9
- down_bias: float32 [256], replicated, may hold values from -3 to 3
- down_weight: bfloat16 [1024, 512], replicated, may hold values from -0.1875 to 0.1875
- down_offset: float32 [512], replicated, may hold values from -3 to 3
Outputs:
- pooled: bfloat16 [128, 16, 512], P(('slide', 'sx'), 'sy'), parts along dimension 0
- grad_features: bfloat16 [1024, 128, 256], P(('slide', 'sx'), 'sy'), parts along dimension 0
- grad_conv_weight: float32 [14, 7, 256], P('slide'), parts along dimension 0
- grad_expand_weight: float32 [512, 1024], P('slide'), parts along dimension 0
- grad_project_weight: float32 [2048, 256], P('slide'), parts along dimension 0
- grad_down_weight: float32 [2048, 512], P('slide'), parts along dimension 0
- grad_vectors: float32 [14, 256], P('slide'), parts along dimension 0
- grad_expand_bias: float32 [2048], P('slide'), parts along dimension 0
- grad_down_offset: float32 [1024], P('slide'), parts along dimension 0
There are 2 independent parts, one for each index of `slide`. A program takes and returns all parts, laid end to end along the dimension named above; an argument that names none is the same for every part. Nothing has to cross between parts.
Inputs may be any that keep to these rules, and one draw needn't show every extreme that they name: `return_slot`: -1 marks a tile position without tissue; otherwise a * 2 + j says that the tile's pooled gradient lies in slot j that the aggregator at sx index a, same sy index, keeps for this owner. On one device no two tiles share a value; every device has 2 or more tissue tiles, and on every device some aggregator fills all 2 of its slots. Slots that no tile names hold values that are not used.
All inputs are finite; a program needn't handle non-finite values.
Results may differ from a plain program's by a relative error of at most 0.0059.
Values may be sent and summed in bfloat16 or wider, within the bound.
A program may use at most 64 MiB of HBM per device.

v0:
```python
import jax
import jax.numpy as jnp
from jax import lax
from jax.sharding import PartitionSpec as P

TILE = 8


norm_eps = 1e-06
gelu_scale = 0.7978845608028654
gelu_cubic = 0.044715


def with_halo(x, sides, width):
    for axis, dim in sides:
        size, length = (lax.axis_size(axis), x.shape[dim])
        up = [(i, (i + 1) % size) for i in range(size - 1)]
        down = [(j, i) for i, j in up]
        last = lax.slice_in_dim(x, length - width, length, axis=dim)
        leading = lax.slice_in_dim(x, 0, width, axis=dim)
        before = lax.ppermute(last, axis, up)
        after = lax.ppermute(leading, axis, down)
        x = jnp.concatenate([before, x, after], axis=dim)
    return x


def gelu_value(hidden):
    inner = gelu_scale * (hidden + gelu_cubic * hidden * hidden * hidden)
    return 0.5 * hidden * (1.0 + jnp.tanh(inner))


def gelu_slope(hidden):
    inner = gelu_scale * (hidden + gelu_cubic * hidden * hidden * hidden)
    tanh_val = jnp.tanh(inner)
    return 0.5 * (1.0 + tanh_val) + 0.5 * hidden * (1.0 - tanh_val * tanh_val) * gelu_scale * (
        1.0 + 3.0 * gelu_cubic * hidden * hidden
    )


def normalize(values):
    centre = jnp.mean(values, axis=-1, keepdims=True)
    shifted = values - centre
    spread = jnp.mean(shifted * shifted, axis=-1, keepdims=True)
    inv_std = lax.rsqrt(spread + norm_eps)
    return (shifted * inv_std, inv_std)


def normalize_back(grad_norm, normed, inv_std):
    first = jnp.mean(grad_norm, axis=-1, keepdims=True)
    second = jnp.mean(grad_norm * normed, axis=-1, keepdims=True)
    return inv_std * (grad_norm - first - normed * second)


def depthwise(padded, kernel, width_x, width_y):
    total = jnp.zeros((width_x, width_y, padded.shape[-1]), jnp.float32)
    for row_off in range(7):
        for col_off in range(7):
            total = (
                total
                + padded[row_off : row_off + width_x, col_off : col_off + width_y]
                * kernel[row_off, col_off]
            )
    return total


def kernel_grad(padded, grad_out):
    width_x, width_y = (grad_out.shape[0], grad_out.shape[1])
    rows_list = []
    for row_off in range(7):
        cols_list = []
        for col_off in range(7):
            window = padded[row_off : row_off + width_x, col_off : col_off + width_y]
            cols_list.append(jnp.sum(window * grad_out, axis=(0, 1)))
        rows_list.append(jnp.stack(cols_list))
    return jnp.stack(rows_list)


def to_patches(grid):
    half_x, half_y, chans = (grid.shape[0] // 2, grid.shape[1] // 2, grid.shape[2])
    return (
        grid.reshape(half_x, 2, half_y, 2, chans)
        .transpose(0, 2, 1, 3, 4)
        .reshape(half_x * half_y, 4 * chans)
    )


def tile_sums(rows, tiles_x, tiles_y, half_tile):
    return rows.reshape(tiles_x, half_tile, tiles_y, half_tile, rows.shape[-1]).sum(axis=(1, 3))


def spread_tiles(per_tile, half_tile, chans):
    tiles_x, tiles_y = (per_tile.shape[0], per_tile.shape[1])
    blocks = per_tile.reshape(tiles_x, tiles_y, 2, 2, chans).transpose(0, 2, 1, 3, 4)
    wide = jnp.broadcast_to(
        blocks[:, None, :, :, None, :, :], (tiles_x, half_tile, 2, tiles_y, half_tile, 2, chans)
    )
    return wide.reshape(tiles_x * half_tile * 2, tiles_y * half_tile * 2, chans)


def input_rim(masked):
    return with_halo(masked, (("sx", 0), ("sy", 1)), 3)


def gradient_rim(grad_conv):
    return with_halo(grad_conv, (("sx", 0), ("sy", 1)), 3)


def fetch_returns(returned_grads):
    arrived = lax.all_to_all(returned_grads, "sx", split_axis=1, concat_axis=1, tiled=True)
    return arrived[0]


def on_device(
    features,
    return_slot,
    returned_grads,
    conv_weight,
    conv_bias,
    norm_gain,
    norm_bias,
    expand_weight,
    expand_bias,
    project_weight,
    project_bias,
    layer_scale,
    down_gain,
    down_bias,
    down_weight,
    down_offset,
):
    tiles_x, tiles_y = return_slot.shape
    width_x, width_y, chans = features.shape
    half_tile = TILE // 2
    tissue = return_slot >= 0
    pixel_mask = jnp.repeat(jnp.repeat(tissue, TILE, axis=0), TILE, axis=1)
    masked = features * pixel_mask[:, :, None].astype(jnp.bfloat16)
    padded_in = input_rim(masked).astype(jnp.float32)
    conv_out = depthwise(padded_in, conv_weight, width_x, width_y) + conv_bias
    normed_conv, inv_conv = normalize(conv_out)
    normed_in = (normed_conv * norm_gain + norm_bias).astype(jnp.bfloat16).reshape(-1, chans)
    hidden = jnp.dot(normed_in, expand_weight, preferred_element_type=jnp.float32) + expand_bias
    active = gelu_value(hidden).astype(jnp.bfloat16)
    branch = (
        jnp.dot(active, project_weight, preferred_element_type=jnp.float32) + project_bias
    ).reshape(width_x, width_y, chans)
    summed = (masked.astype(jnp.float32) + layer_scale * branch).astype(jnp.bfloat16)
    normed_sum, inv_sum = normalize(summed.astype(jnp.float32))
    down_in = (normed_sum * down_gain + down_bias).astype(jnp.bfloat16)
    patches = to_patches(down_in)
    reduced = jnp.dot(patches, down_weight, preferred_element_type=jnp.float32) + down_offset
    tissue_f = tissue[:, :, None].astype(jnp.float32)
    pooled = (
        tile_sums(reduced, tiles_x, tiles_y, half_tile) / (half_tile * half_tile) * tissue_f
    ).astype(jnp.bfloat16)
    arrived = fetch_returns(returned_grads)
    selector = (
        return_slot.reshape(-1)[:, None] == jnp.arange(arrived.shape[0], dtype=jnp.int32)[None, :]
    ).astype(jnp.bfloat16)
    grad_pool = jnp.dot(selector, arrived, preferred_element_type=jnp.float32).reshape(
        tiles_x, tiles_y, -1
    )
    grad_reduced = grad_pool / (half_tile * half_tile)
    grad_reduced_b = grad_reduced.astype(jnp.bfloat16)
    patch_sums = tile_sums(patches.astype(jnp.float32), tiles_x, tiles_y, half_tile)
    grad_down_weight = lax.dot_general(
        patch_sums.reshape(-1, 4 * chans),
        grad_reduced.reshape(-1, grad_reduced.shape[-1]),
        (((0,), (0,)), ((), ())),
        precision=lax.Precision.HIGHEST,
        preferred_element_type=jnp.float32,
    )
    grad_down_offset = jnp.sum(grad_pool, axis=(0, 1))
    grad_patch = lax.dot_general(
        grad_reduced_b, down_weight, (((2,), (1,)), ((), ())), preferred_element_type=jnp.float32
    )
    grad_down_in = spread_tiles(grad_patch, half_tile, chans)
    grad_down_gain = jnp.sum(grad_down_in * normed_sum, axis=(0, 1))
    grad_down_bias = jnp.sum(grad_down_in, axis=(0, 1))
    grad_summed = normalize_back(grad_down_in * down_gain, normed_sum, inv_sum)
    grad_scale = jnp.sum(grad_summed * branch, axis=(0, 1))
    grad_branch = layer_scale * grad_summed
    grad_project_bias = jnp.sum(grad_branch, axis=(0, 1))
    grad_branch_b = grad_branch.reshape(-1, chans).astype(jnp.bfloat16)
    grad_project_weight = lax.dot_general(
        active, grad_branch_b, (((0,), (0,)), ((), ())), preferred_element_type=jnp.float32
    )
    grad_active = lax.dot_general(
        grad_branch_b, project_weight, (((1,), (1,)), ((), ())), preferred_element_type=jnp.float32
    )
    grad_hidden = grad_active * gelu_slope(hidden)
    grad_expand_bias = jnp.sum(grad_hidden, axis=0)
    grad_hidden_b = grad_hidden.astype(jnp.bfloat16)
    grad_expand_weight = lax.dot_general(
        normed_in, grad_hidden_b, (((0,), (0,)), ((), ())), preferred_element_type=jnp.float32
    )
    grad_normed_in = lax.dot_general(
        grad_hidden_b, expand_weight, (((1,), (1,)), ((), ())), preferred_element_type=jnp.float32
    ).reshape(width_x, width_y, chans)
    grad_norm_gain = jnp.sum(grad_normed_in * normed_conv, axis=(0, 1))
    grad_norm_bias = jnp.sum(grad_normed_in, axis=(0, 1))
    grad_conv = normalize_back(grad_normed_in * norm_gain, normed_conv, inv_conv)
    grad_conv_bias = jnp.sum(grad_conv, axis=(0, 1))
    grad_conv_weight = kernel_grad(padded_in, grad_conv)
    padded_grad = gradient_rim(grad_conv)
    grad_in = depthwise(padded_grad, conv_weight[::-1, ::-1], width_x, width_y)
    grad_features = ((grad_summed + grad_in) * pixel_mask[:, :, None].astype(jnp.float32)).astype(
        jnp.bfloat16
    )
    totals = lax.psum(
        (
            grad_down_weight,
            grad_down_offset,
            grad_down_gain,
            grad_down_bias,
            grad_scale,
            grad_project_bias,
            grad_expand_weight,
            grad_project_weight,
            grad_expand_bias,
            grad_norm_gain,
            grad_norm_bias,
            grad_conv_weight,
            grad_conv_bias,
        ),
        ("sx", "sy"),
    )
    (
        sum_down_weight,
        sum_down_offset,
        sum_down_gain,
        sum_down_bias,
        sum_scale,
        sum_project_bias,
        sum_expand_weight,
        sum_project_weight,
        sum_expand_bias,
        sum_norm_gain,
        sum_norm_bias,
        sum_conv_weight,
        sum_conv_bias,
    ) = totals
    grad_vectors = jnp.stack(
        [
            sum_conv_bias,
            sum_norm_gain,
            sum_norm_bias,
            sum_project_bias,
            sum_scale,
            sum_down_gain,
            sum_down_bias,
        ]
    )
    return (
        pooled,
        grad_features,
        sum_conv_weight,
        sum_expand_weight,
        sum_project_weight,
        sum_down_weight,
        grad_vectors,
        sum_expand_bias,
        sum_down_offset,
    )


def solution(mesh):
    placed = (
        P(("slide", "sx"), "sy", None),
        P(("slide", "sx"), "sy"),
        P("sy", ("slide", "sx"), None),
        P(),
        P(),
        P(),
        P(),
        P(),
        P(),
        P(),
        P(),
        P(),
        P(),
        P(),
        P(),
        P(),
    )
    return jax.shard_map(
        on_device,
        mesh=mesh,
        in_specs=placed,
        out_specs=(
            P(("slide", "sx"), "sy", None),
            P(("slide", "sx"), "sy", None),
            P("slide", None, None),
            P("slide", None),
            P("slide", None),
            P("slide", None),
            P("slide", None),
            P("slide"),
            P("slide"),
        ),
        check_vma=False,
    )
```

profile of v0, /device:TPU:1, one launch (start us, length us, event | category | flops | bytes accessed | tf_op | source)
XLA Modules:
  0.0 665.5 jit_solution(5076684166615677596)
XLA Ops:
  8.4 1.2 broadcast_multiply_fusion
  9.6 4.5 collective-permute-start
  14.1 1.9 collective-permute-start.1
  18.9 6.0 all-to-all-start
  25.0 1.6 fusion.103
  26.7 1.7 fusion.104
  28.4 1.5 fusion.105
  30.9 1.5 fusion.107
  32.8 1.4 broadcast_reduce_fusion
  34.3 3.5 collective-permute-start.2
  37.8 1.3 collective-permute-start.3
  39.6 1.7 reshape.162
  41.5 1.6 collective-permute-done.3
  43.6 9.0 %fusion.100 = (f32[32,32]{1,0:T(8,128)S(1)}, f32[32,32,256]{2,1,0:T(8,128)S(1)}) fusion(f32[256]{0:T(256)} %param.20, f32[256]{0:T(256)} %bitcast.280, f32[38,38,256]{2,1,0:T(8,128)S(1)} %maximum_convert_fusion, f32[256]{0:T(256)} %bitcast.282, f32[256]{0:T(256)S(1)} %bitcast.188, f32[256]{0:T(256)S(1)} %bitcast.190, f32[256]{0:T(256)S(1)} %bitcast.192, ...), kind=kLoop, calls=%fused_computation.255 | loop fusion | flops 25951232 | bytes 52484096 | tf_op jit(solution)/shard_map/reduce_sum | solution.py:41
  54.1 1.8 multiply_convert_fusion
  59.1 2.2 multiply_reduce_fusion
  61.3 3.8 fusion.106
  65.2 1.3 fusion.98
  67.6 4.9 multiply_reduce_fusion.2
  72.4 3.0 multiply_reduce_fusion.20
  75.5 2.6 multiply_reduce_fusion.38
  78.1 1.7 fusion.108
  79.8 1.7 fusion.81
  81.8 1.5 fusion.97
  83.2 2.0 reshape.164
  85.2 1.6 reduce_sum.670
  86.8 3.2 convolution_bitcast_fusion
  90.0 1.2 copy-done.2
  91.9 4.8 collective-permute-start.4
  96.7 1.9 collective-permute-start.5
  98.6 1.4 reshape.159
  102.9 1.3 stack.241
  104.2 1.3 stack.232
  105.5 1.3 stack.223
  106.8 1.3 constant_dynamic-update-slice_fusion.6
  108.1 1.3 constant_dynamic-update-slice_fusion.5
  109.4 1.3 constant_dynamic-update-slice_fusion.4
  112.5 1.9 convolution_add_fusion.1
  115.0 1.2 reshape.160
  116.4 272.5 %all-reduce = (f32[7,7,256]{2,1,0:T(8,128)}, f32[1,256]{1,0:T(1,128)S(1)}, f32[1,256]{1,0:T(1,128)S(1)}, f32[1,256]{1,0:T(1,128)S(1)}, f32[1,256]{1,0:T(1,128)S(...) all-reduce(f32[7,7,256]{2,1,0:T(8,128)} %constant_dynamic-update-sl, ...), channel_id=1, replica_groups=mesh['slide'=2,'sx'=16,'sy'=4] {'sx','sy'}, use_global_device_ids=true, to_apply=%region_58.0 | all-reduce | flops 15872 | bytes 126976 | tf_op jit(solution)/shard_map/psum | solution.py:209
  389.5 1.3 collective-permute-start.6
  390.8 1.3 collective-permute-start.7
  392.1 1.4 multiply_convert_fusion.2
  393.9 3.9 collective-permute-done.7
  398.4 11.6 %fusion.85 = bf16[32,32,256]{2,1,0:T(8,128)(2,1)} fusion(f32[38,35,256]{2,1,0:T(8,128)S(1)} %get-tuple-element.90, f32[3,32,256]{2,1,0:T(8,128)S(1)} %collective-permute-done.5, f32[32,32,256]{2,1,0:T(8,128)S(1)} %copy-done.2, f32[38,35,256]{2,1,0:T(8,128)S(1)} %get-tuple-element.89, f32[3,32,256]{2,1,0:T(8,128)S(1)} %collective-permute-done.4, ...), kind=kLoop, calls=%fused_computation.206 | loop fusion | flops 29884416 | bytes 47454208 | tf_op jit(solution)/shard_map/convert_element_type | solution.py:206
  410.0 243.9 %all-reduce.4.cloned.1.call-done = (f32[256,1024]{1,0:T(8,128)}, f32[1024,256]{1,0:T(8,128)}, f32[1024,512]{1,0:T(8,128)}) async-done(((f32[256,1024]{1,0:T(8,128)}, f32[1024,256]{1,0:T(8,128)}, f32[1024,512]{1,0:T(8,128)}), (f32[256,1024]{1,0:T(8,128)}, f32[1024,256]{1,0:T(8,128)}, f32[1024,512]{1,0:T(8,128)})) %all-reduce.4.cloned.1.call-update) | async-done | bytes 4194320 | tf_op jit(solution)/shard_map/psum | solution.py:209
  653.9 2.5 copy.74
  657.3 1.3 copy.76
  (237 shorter events, 20.4 us)
Async XLA Ops:
  7.2 25.2 %copy-start = (bf16[1024,512]{1,0:T(8,128)(2,1)S(1)}, bf16[1024,512]{1,0:T(8,128)(2,1)}, u32[]{:S(2)}) copy-start(bf16[1024,512]{1,0:T(8,128)(2,1)} %param.30) | copy-start | bytes 3145732
  7.2 25.6 %copy-start.17 = (f32[256]{0:T(256)S(1)}, f32[256]{0:T(256)}, u32[]{:S(2)}) copy-start(f32[256]{0:T(256)} %param.28) | copy-start | bytes 3076
  9.6 24.6 %collective-permute-start = (bf16[3,32,256]{2,1,0:T(8,128)(2,1)S(1)}, bf16[3,32,256]{2,1,0:T(8,128)(2,1)S(1)}, u32[]{:S(2)}, u32[]{:S(2)}) collective-permute-start(bf16[3,32,256]{2,1,0:T(8,128)(2,1)S(1)} %get-tuple-element.100), channel_id=1, source_target_pairs={{0,4},{4,8},{8,12},{12,16},{16,20},{20,24},{24,28},{28,32},{32,36}... | collective-permute-start | bytes 147464 | tf_op jit(solution)/shard_map/ppermute | solution.py:21
  14.1 20.0 %collective-permute-start.1 = (bf16[3,32,256]{2,1,0:T(8,128)(2,1)S(1)}, bf16[3,32,256]{2,1,0:T(8,128)(2,1)S(1)}, u32[]{:S(2)}, u32[]{:S(2)}) collective-permute-start(bf16[3,32,256]{2,1,0:T(8,128)(2,1)S(1)} %get-tuple-element.101), channel_id=1, source_target_pairs={{4,0},{8,4},{12,8},{16,12},{20,16},{24,20},{28,24},{32,28},{36,32}... | collective-permute-start | bytes 147464 | tf_op jit(solution)/shard_map/ppermute | solution.py:22
  18.9 12.0 %all-to-all-start = ((bf16[16,2,512]{2,1,0:T(2,128)(2,1)}), bf16[16,2,512]{2,1,0:T(2,128)(2,1)S(1)}, u32[]{:S(2)}, u32[]{:S(2)}) async-start(bf16[16,2,512]{2,1,0:T(2,128)(2,1)} %reshape.169), calls=%async_computation | async-start | bytes 65536 | tf_op jit(solution)/shard_map/all_to_all | solution.py:109
  24.9 629.0 %all-reduce.4.cloned.1.call-start = ((), (), s32[]{:S(2)}) async-start(), calls=%async_computation.1 | async-start | bytes 8388608 | tf_op jit(solution)/shard_map/psum | solution.py:209
  26.5 16.9 %copy-start.19 = (f32[1,1,256]{2,1,0:T(1,128)}, f32[1,1,256]{2,1,0:T(1,128)S(1)}, u32[]{:S(2)}) copy-start(f32[1,1,256]{2,1,0:T(1,128)S(1)} %get-tuple-element.102) | copy-start | bytes 3076
  26.5 16.9 %copy-start.21 = (f32[1,1,256]{2,1,0:T(1,128)}, f32[1,1,256]{2,1,0:T(1,128)S(1)}, u32[]{:S(2)}) copy-start(f32[1,1,256]{2,1,0:T(1,128)S(1)} %get-tuple-element.103) | copy-start | bytes 3076
  26.5 16.9 %copy-start.23 = (f32[1,1,256]{2,1,0:T(1,128)}, f32[1,1,256]{2,1,0:T(1,128)S(1)}, u32[]{:S(2)}) copy-start(f32[1,1,256]{2,1,0:T(1,128)S(1)} %get-tuple-element.104) | copy-start | bytes 3076
  26.6 16.9 %copy-start.25 = (f32[1,1,256]{2,1,0:T(1,128)}, f32[1,1,256]{2,1,0:T(1,128)S(1)}, u32[]{:S(2)}) copy-start(f32[1,1,256]{2,1,0:T(1,128)S(1)} %get-tuple-element.105) | copy-start | bytes 3076
  26.6 16.9 %copy-start.27 = (f32[1,1,256]{2,1,0:T(1,128)}, f32[1,1,256]{2,1,0:T(1,128)S(1)}, u32[]{:S(2)}) copy-start(f32[1,1,256]{2,1,0:T(1,128)S(1)} %get-tuple-element.106) | copy-start | bytes 3076
  26.6 16.9 %copy-start.29 = (f32[1,1,256]{2,1,0:T(1,128)}, f32[1,1,256]{2,1,0:T(1,128)S(1)}, u32[]{:S(2)}) copy-start(f32[1,1,256]{2,1,0:T(1,128)S(1)} %get-tuple-element.107) | copy-start | bytes 3076
  26.6 16.9 %copy-start.31 = (f32[1,1,256]{2,1,0:T(1,128)}, f32[1,1,256]{2,1,0:T(1,128)S(1)}, u32[]{:S(2)}) copy-start(f32[1,1,256]{2,1,0:T(1,128)S(1)} %get-tuple-element.108) | copy-start | bytes 3076
  26.6 16.9 %copy-start.33 = (f32[1,1,256]{2,1,0:T(1,128)}, f32[1,1,256]{2,1,0:T(1,128)S(1)}, u32[]{:S(2)}) copy-start(f32[1,1,256]{2,1,0:T(1,128)S(1)} %get-tuple-element.109) | copy-start | bytes 3076
  26.6 16.9 %copy-start.35 = (f32[1,1,256]{2,1,0:T(1,128)}, f32[1,1,256]{2,1,0:T(1,128)S(1)}, u32[]{:S(2)}) copy-start(f32[1,1,256]{2,1,0:T(1,128)S(1)} %get-tuple-element.110) | copy-start | bytes 3076
  26.6 16.9 %copy-start.37 = (f32[1,1,256]{2,1,0:T(1,128)}, f32[1,1,256]{2,1,0:T(1,128)S(1)}, u32[]{:S(2)}) copy-start(f32[1,1,256]{2,1,0:T(1,128)S(1)} %get-tuple-element.111) | copy-start | bytes 3076
  26.6 16.9 %copy-start.39 = (f32[1,1,256]{2,1,0:T(1,128)}, f32[1,1,256]{2,1,0:T(1,128)S(1)}, u32[]{:S(2)}) copy-start(f32[1,1,256]{2,1,0:T(1,128)S(1)} %get-tuple-element.112) | copy-start | bytes 3076
  26.6 16.9 %copy-start.41 = (f32[1,1,256]{2,1,0:T(1,128)}, f32[1,1,256]{2,1,0:T(1,128)S(1)}, u32[]{:S(2)}) copy-start(f32[1,1,256]{2,1,0:T(1,128)S(1)} %get-tuple-element.113) | copy-start | bytes 3076
  26.6 16.9 %copy-start.43 = (f32[1,1,256]{2,1,0:T(1,128)}, f32[1,1,256]{2,1,0:T(1,128)S(1)}, u32[]{:S(2)}) copy-start(f32[1,1,256]{2,1,0:T(1,128)S(1)} %get-tuple-element.114) | copy-start | bytes 3076
  26.7 16.9 %copy-start.45 = (f32[1,1,256]{2,1,0:T(1,128)}, f32[1,1,256]{2,1,0:T(1,128)S(1)}, u32[]{:S(2)}) copy-start(f32[1,1,256]{2,1,0:T(1,128)S(1)} %get-tuple-element.115) | copy-start | bytes 3076
  26.7 16.9 %copy-start.47 = (f32[1,1,256]{2,1,0:T(1,128)}, f32[1,1,256]{2,1,0:T(1,128)S(1)}, u32[]{:S(2)}) copy-start(f32[1,1,256]{2,1,0:T(1,128)S(1)} %get-tuple-element.116) | copy-start | bytes 3076
  26.7 16.9 %copy-start.49 = (f32[1,1,256]{2,1,0:T(1,128)}, f32[1,1,256]{2,1,0:T(1,128)S(1)}, u32[]{:S(2)}) copy-start(f32[1,1,256]{2,1,0:T(1,128)S(1)} %get-tuple-element.117) | copy-start | bytes 3076
  34.3 7.3 %collective-permute-start.2 = (bf16[38,3,256]{2,1,0:T(4,128)(2,1)S(1)}, bf16[38,3,256]{2,1,0:T(4,128)(2,1)S(1)}, u32[]{:S(2)}, u32[]{:S(2)}) collective-permute-start(bf16[38,3,256]{2,1,0:T(4,128)(2,1)S(1)} %get-tuple-element.95), channel_id=1, source_target_pairs={{0,1},{1,2},{2,3},{4,5},{5,6},{6,7},{8,9},{9,10},{10,11},{12,13},{... | collective-permute-start | bytes 175112 | tf_op jit(solution)/shard_map/ppermute | solution.py:21
  37.8 5.3 collective-permute-start.3
  43.6 9.5 %copy-start.76 = (f32[256]{0:T(256)S(1)}, f32[256]{0:T(256)}, u32[]{:S(2)}) copy-start(f32[256]{0:T(256)} %param.21) | copy-start | bytes 3076
  43.6 9.5 %copy-start.78 = (f32[256]{0:T(256)S(1)}, f32[256]{0:T(256)}, u32[]{:S(2)}) copy-start(f32[256]{0:T(256)} %param.22) | copy-start | bytes 3076
  52.7 13.8 %copy-start.3 = (f32[32,32,256]{2,1,0:T(8,128)}, f32[32,32,256]{2,1,0:T(8,128)S(1)}, u32[]{:S(2)}) copy-start(f32[32,32,256]{2,1,0:T(8,128)S(1)} %get-tuple-element.87) | copy-start | bytes 3145732
  91.9 297.6 %collective-permute-start.4 = (f32[3,32,256]{2,1,0:T(8,128)}, f32[3,32,256]{2,1,0:T(8,128)S(1)}, u32[]{:S(2)}, u32[]{:S(2)}) collective-permute-start(f32[3,32,256]{2,1,0:T(8,128)} %get-tuple-element.93), channel_id=1, source_target_pairs={{0,4},{4,8},{8,12},{12,16},{16,20},{20,24},{24,28},{28,32},{32,36}... | collective-permute-start | bytes 294920 | tf_op jit(solution)/shard_map/ppermute | solution.py:21
  96.7 292.8 %collective-permute-start.5 = (f32[3,32,256]{2,1,0:T(8,128)S(1)}, f32[3,32,256]{2,1,0:T(8,128)S(1)}, u32[]{:S(2)}, u32[]{:S(2)}) collective-permute-start(f32[3,32,256]{2,1,0:T(8,128)S(1)} %get-tuple-element.94), channel_id=1, source_target_pairs={{4,0},{8,4},{12,8},{16,12},{20,16},{24,20},{28,24},{32,28},{36,32}... | collective-permute-start | bytes 294920 | tf_op jit(solution)/shard_map/ppermute | solution.py:22
  389.5 4.3 collective-permute-start.6
  390.8 7.0 %collective-permute-start.7 = (f32[38,3,256]{2,1,0:T(4,128)S(1)}, f32[38,3,256]{2,1,0:T(4,128)S(1)}, u32[]{:S(2)}, u32[]{:S(2)}) collective-permute-start(f32[38,3,256]{2,1,0:T(4,128)S(1)} %get-tuple-element.92), channel_id=1, source_target_pairs={{1,0},{2,1},{3,2},{5,4},{6,5},{7,6},{9,8},{10,9},{11,10},{13,12},{... | collective-permute-start | bytes 350216 | tf_op jit(solution)/shard_map/ppermute | solution.py:22
  393.5 4.6 copy-start.24
  393.5 4.6 copy-start.26
  393.5 4.6 copy-start.28
  393.5 4.6 copy-start.30
  393.5 4.6 copy-start.32
  393.5 4.6 copy-start.34
  393.5 4.6 copy-start.36
  393.6 4.6 copy-start.38
  393.6 4.6 copy-start.40
  393.6 4.6 copy-start.42
  393.6 4.6 copy-start.44
  393.6 4.6 copy-start.46
  393.6 4.6 copy-start.48
  393.6 4.6 copy-start.50
  393.6 4.6 copy-start.52
  393.6 4.6 copy-start.54
  393.6 4.6 copy-start.56
  (48 other events, 160.5 us)
Sparse Core Ops, SparseCore 0:
  90.1 563.7 all-reduce.3
where the time goes:
time: 668 us; the launch traced here: 666 us
  blocking collectives  272 us (41%)
  waiting for transfers between devices  249 us (37%)
  other arithmetic  46.6 us (7%)
  local copies, waits for them, and re-layouts  36.9 us (6%)
  starting transfers between devices  26.7 us (4%)
  matrix products  18.1 us (3%)
  between operations  15.4 us (2%)
    psum x1, blocking collectives, on_device(): lax.psum((grad_down_weight, grad_down_offset, grad_down_gain, grad_down_b...  272 us
    psum x1, waiting for transfers between devices, on_device(): lax.psum((grad_down_weight, grad_down_offset, grad_down_gain, grad_down_b...  244 us
    unnamed x185, local copies, waits for them, and re-layouts  15.5 us
    ppermute x4, starting transfers between devices, with_halo(): before = lax.ppermute(last, axis, up)  14.1 us
  transfers between devices with their start and end apart: 10, of which 3 were waited for; matrix products, arithmetic and copies ran while one was open for 7% of the time, Pallas kernels for 0%

commit v1 on v0

v1 whole, which is shorter than its diff:
```python
import functools

import jax
import jax.numpy as jnp
from jax import lax
from jax.experimental import pallas as pl
from jax.experimental.pallas import tpu as pltpu
from jax.sharding import PartitionSpec as P

F32 = jnp.float32
BF16 = jnp.bfloat16
MESH = pl.DeviceIdType.MESH

norm_eps = 1e-06
gelu_scale = 0.7978845608028654
gelu_cubic = 0.044715

WX = 32
WY = 32
LEFT = 8
PITCH = 48
PLANE = 38 * PITCH
N_SX = 16
N_SY = 4


def mm(a, b, ca, cb):
    return lax.dot_general(a, b, (((ca,), (cb,)), ((), ())), preferred_element_type=F32)


def fold8(v):
    return jnp.sum(v.reshape(v.shape[0] // 8, 8, v.shape[1]), axis=0)


def row_mean(v):
    return jnp.sum(v, axis=-1, keepdims=True) * (1.0 / v.shape[-1])


def kernel(
    slot_ref, feat_ref, ret_ref, cw_ref, cb_ref, ng_ref, nb_ref, w1_ref, b1_ref, w2_ref, b2_ref, ls_ref, dg_ref,
    db_ref, dw_ref, do_ref,
    pooled_ref, gf_ref, small_ref, big_ref,
    p_ref, pg_ref, yp_ref, yr_ref, cr_ref, wb_ref, mn_ref, mv_ref,
    rg_ref, pk_ref, rv_ref, ar_ref, gr_ref, gp_ref, ps_ref,
    co_ref, nc_ref, inv_ref, ni_ref, act_ref, sl_ref, gs_ref, gb_ref, nat_ref,
    kg_ref, v_ref, vr_ref, vz_ref, vf_ref,
    loc_ref, s0_ref, r0_ref, t0_ref, r1_ref, t1_ref, r2_ref, t2_ref, r3_ref, fin_ref,
    hs_sem, hr_sem, as_sem, ar_sem, bs_sem, br_sem, vs_sem, vr_sem, out_sem,
):
    sx = lax.axis_index("sx")
    sy = lax.axis_index("sy")
    core = lax.rem(sx, 2)
    xl = lax.rem(sx // 2, 2)
    yy = sx // 4

    def at_sx(k):
        return lax.rem(sx + k + N_SX, N_SX)

    def at_sy(k):
        return lax.rem(sy + k + N_SY, N_SY)

    barrier = pltpu.get_barrier_semaphore()

    def greet(k, c):
        pl.semaphore_signal(barrier, inc=1, device_id={"sx": at_sx(k)}, device_id_type=MESH)
        return c

    lax.fori_loop(1, N_SX, greet, 0)
    for k in range(1, N_SY):
        pl.semaphore_signal(barrier, inc=1, device_id={"sy": at_sy(k)}, device_id_type=MESH)
    for i in (-1, 1):
        for j in (-1, 1):
            pl.semaphore_signal(barrier, inc=1, device_id={"sx": at_sx(i), "sy": at_sy(j)}, device_id_type=MESH)

    sub = lax.broadcasted_iota(jnp.int32, (8, 128), 0)
    lane = lax.broadcasted_iota(jnp.int32, (8, 128), 1)
    sel = []
    for tx in range(4):
        picked = jnp.zeros((8, 128), jnp.int32)
        for ty in range(4):
            s = slot_ref[tx, ty]
            picked = jnp.where(sub // 2 == ty, s, picked)
            mn_ref[tx, ty * 8 : ty * 8 + 8, :] = jnp.where(jnp.full((8, 128), s) >= 0, 1.0, 0.0).astype(F32)
        mv_ref[tx] = jnp.where(picked >= 0, 1.0, 0.0).astype(F32)
        sel.append(jnp.where(picked == lane, 1.0, 0.0).astype(F32))
    selector = jnp.concatenate(sel, axis=0).astype(BF16)[:, :32]

    def fill(x, c):
        f = feat_ref[x].astype(F32)
        m = mn_ref[x // 8]
        at = pl.multiple_of((x + 3) * PITCH + LEFT, 8)
        for h in range(2):
            p_ref[h, pl.ds(at, WY), :] = f[:, h * 128 : h * 128 + 128] * m
        return c

    lax.fori_loop(0, WX, fill, 0)

    def pack(e, ref):
        for side, col in ((0, 0), (1, WY - 3)):
            for h in range(2):
                for c in range(3):
                    for g in range(4):
                        yp_ref[e, side, h, c, g * 8 : g * 8 + 8, :] = ref[
                            h, pl.ds((3 + g * 8) * PITCH + LEFT + col + c, 8, stride=PITCH), :
                        ]

    def halo_copies(e, ref):
        def rc(src, dst, k, dev):
            return pltpu.make_async_remote_copy(
                src_ref=src, dst_ref=dst, send_sem=hs_sem.at[e, k], recv_sem=hr_sem.at[e, k], device_id=dev,
                device_id_type=MESH,
            )

        out = [
            rc(ref.at[:, 3 * PITCH : 6 * PITCH, :], ref.at[:, 35 * PITCH : 38 * PITCH, :], 0, {"sx": at_sx(-1)}),
            rc(ref.at[:, 32 * PITCH : 35 * PITCH, :], ref.at[:, 0 : 3 * PITCH, :], 1, {"sx": at_sx(1)}),
        ]
        for side, step in ((0, -1), (1, 1)):
            out.append(rc(yp_ref.at[e, side], yr_ref.at[e, side], 2 + side, {"sy": at_sy(step)}))
            out.append(
                rc(yp_ref.at[e, side, :, :, 24:32, :], cr_ref.at[e, 2 * side], 4 + 2 * side,
                   {"sx": at_sx(1), "sy": at_sy(step)})
            )
            out.append(
                rc(yp_ref.at[e, side, :, :, 0:8, :], cr_ref.at[e, 2 * side + 1], 5 + 2 * side,
                   {"sx": at_sx(-1), "sy": at_sy(step)})
            )
        return out

    def unpack(e, ref):
        has_top = sx > 0
        has_bottom = sx < N_SX - 1

        @pl.when(jnp.logical_not(has_top))
        def _():
            ref[:, 0 : 3 * PITCH, :] = jnp.zeros((2, 3 * PITCH, 128), F32)

        @pl.when(jnp.logical_not(has_bottom))
        def _():
            ref[:, 35 * PITCH : 38 * PITCH, :] = jnp.zeros((2, 3 * PITCH, 128), F32)

        for side, col, inside in ((0, LEFT + WY, sy < N_SY - 1), (1, LEFT - 3, sy > 0)):
            keep = jnp.where(inside, 1.0, 0.0).astype(F32)
            keep_top = jnp.where(jnp.logical_and(inside, has_top), 1.0, 0.0).astype(F32)
            keep_bottom = jnp.where(jnp.logical_and(inside, has_bottom), 1.0, 0.0).astype(F32)
            for h in range(2):
                for c in range(3):
                    for g in range(4):
                        ref[h, pl.ds((3 + g * 8) * PITCH + col + c, 8, stride=PITCH), :] = (
                            yr_ref[e, side, h, c, g * 8 : g * 8 + 8, :] * keep
                        )
                    ref[h, pl.ds(col + c, 3, stride=PITCH), :] = cr_ref[e, 2 * side, h, c, 5:8, :] * keep_top
                    ref[h, pl.ds(35 * PITCH + col + c, 3, stride=PITCH), :] = (
                        cr_ref[e, 2 * side + 1, h, c, 0:3, :] * keep_bottom
                    )

    pack(0, p_ref)

    for q in range(4):
        rg_ref[q] = ret_ref[:, q * 128 : q * 128 + 128].astype(F32)
    for q in range(4):
        for s in range(2):
            pk_ref[pl.ds(2 * q + s, 16, stride=8), :] = rg_ref[q, pl.ds(s, 16, stride=2), :]

    pl.semaphore_wait(barrier, (N_SX - 1) + (N_SY - 1) + 4)

    for copy in halo_copies(0, p_ref):
        copy.start()

    def block8(i):
        return pl.ds(pl.multiple_of(i * 8, 8), 8)

    def return_copy(k):
        return pltpu.make_async_remote_copy(
            src_ref=pk_ref.at[block8(at_sx(k))], dst_ref=rv_ref.at[block8(sx)], send_sem=as_sem.at[k],
            recv_sem=ar_sem.at[k], device_id={"sx": at_sx(k)}, device_id_type=MESH,
        )

    def start_return(k, c):
        return_copy(k).start()
        return c

    lax.fori_loop(1, N_SX, start_return, 0)
    rv_ref[block8(sx), :] = pk_ref[block8(sx), :]

    for h in range(2):
        for a in range(7):
            for b in range(7):
                wb_ref[h, a * 7 + b] = jnp.broadcast_to(cw_ref[a, b : b + 1, h * 128 : h * 128 + 128], (8, 128))

    def wait_return(k, c):
        return_copy(k).wait()
        return c

    lax.fori_loop(1, N_SX, wait_return, 0)
    for q in range(4):
        for s in range(2):
            ar_ref[q, pl.ds(s, 16, stride=2), :] = rv_ref[pl.ds(2 * q + s, 16, stride=8), :]
    arrived = jnp.concatenate([ar_ref[q] for q in range(4)], axis=1).astype(BF16)
    grad_pool = mm(selector, arrived, 1, 0)
    grad_reduced = (grad_pool * (1.0 / 16.0)).astype(BF16)
    gr_ref[...] = grad_reduced
    grad_patch = mm(grad_reduced, dw_ref[...], 1, 1)
    for tx in range(4):
        gp_ref[tx] = grad_patch[tx * 8 : tx * 8 + 8, :]

    def clear(i, c):
        loc_ref[1, pl.ds(pl.multiple_of(i * 128, 128), 128), :] = jnp.zeros((128, 256), F32)
        return c

    lax.fori_loop(0, 16, clear, 0)

    kg_ref[...] = jnp.zeros_like(kg_ref)

    def add_entry(t, value):
        for h in range(2):
            kg_ref[h, t * 8 : t * 8 + 8, :] += value[:, h * 128 : h * 128 + 128]

    off_sum = jnp.sum(grad_pool.reshape(4, 8, 512), axis=0) * 0.5
    for q in range(2):
        add_entry(60 + q, off_sum[:, q * 256 : q * 256 + 256])
    bias_sum = jnp.sum(gp_ref[...], axis=0)
    bias_sum = (
        bias_sum[:, 0:256] + bias_sum[:, 256:512] + bias_sum[:, 512:768] + bias_sum[:, 768:1024]
    ) * 8.0
    add_entry(55, bias_sum)

    def plane_rows(ref, h, x, n):
        return [ref[h, pl.ds(x * PITCH + (LEFT - 3) + c, 8, stride=4), :] for c in range(n)]

    def depthwise(ref, h, x, flipped):
        sums = [[None] * 4 for _ in range(2)]
        for r in range(8):
            rows = plane_rows(ref, h, x + r, 10)
            for i in range(2):
                a = r - i
                if a < 0 or a > 6:
                    continue
                for b in range(7):
                    t = a * 7 + b
                    w = wb_ref[h, 48 - t if flipped else t]
                    for c in range(4):
                        term = rows[c + b] * w
                        sums[i][c] = term if sums[i][c] is None else sums[i][c] + term
        return sums

    for copy in halo_copies(0, p_ref):
        copy.wait()
    unpack(0, p_ref)

    def conv_step(i, c):
        x = i * 2
        for h in range(2):
            bias = cb_ref[:, h * 128 : h * 128 + 128]
            sums = depthwise(p_ref, h, x, False)
            for k in range(2):
                for q in range(4):
                    co_ref[h, block8((x + k) * 4 + q), :] = sums[k][q] + bias
        return c

    lax.fori_loop(0, WX // 2, conv_step, 0)

    r32 = lax.broadcasted_iota(jnp.int32, (32, 256), 0)
    k32 = lax.broadcasted_iota(jnp.int32, (32, 256), 1)
    off_of = (k32 // 32 % 2) * 2 + (k32 // 8 % 4) % 2
    patch_sel = jnp.where(
        (off_of == r32 // 8) & (k32 % 8 // 2 == r32 % 8 // 2) & (r32 % 2 == 0), 1.0, 0.0
    ).astype(BF16)

    def spread(blocks):
        row = [blocks[0], blocks[1]] * 2 + [blocks[2], blocks[3]] * 2
        return jnp.concatenate(row * 4, axis=0)

    def forward(tx, c):
        rows = pl.ds(pl.multiple_of(tx * 256, 256), 256)
        v = jnp.concatenate([co_ref[0, rows, :], co_ref[1, rows, :]], axis=1)
        shifted = v - row_mean(v)
        inv = lax.rsqrt(row_mean(shifted * shifted) + norm_eps)
        normed = shifted * inv
        nc_ref[rows, :] = normed
        inv_ref[rows, :] = jnp.broadcast_to(inv, (256, 128))
        normed_in = (normed * ng_ref[...] + nb_ref[...]).astype(BF16)
        ni_ref[rows, :] = normed_in
        branch = None
        for j in range(4):
            cols = slice(j * 256, j * 256 + 256)
            hid = mm(normed_in, w1_ref[:, cols], 1, 0) + b1_ref[:, cols]
            sq = hid * hid
            t = jnp.tanh(hid * (gelu_scale + (gelu_scale * gelu_cubic) * sq))
            u = 0.5 + 0.5 * t
            act = (hid * u).astype(BF16)
            act_ref[rows, cols] = act
            sl_ref[rows, cols] = u + hid * (u - u * t) * (gelu_scale + (3.0 * gelu_scale * gelu_cubic) * sq)
            part = mm(act, w2_ref[cols, :], 1, 0)
            branch = part if branch is None else branch + part
        branch = branch + b2_ref[...]
        masked = jnp.concatenate(
            [
                jnp.concatenate(
                    [
                        p_ref[h, pl.ds((tx * 8 + x + 3) * PITCH + LEFT + q, 8, stride=4), :]
                        for x in range(8)
                        for q in range(4)
                    ],
                    axis=0,
                )
                for h in range(2)
            ],
            axis=1,
        )
        summed = (masked + ls_ref[...] * branch).astype(BF16).astype(F32)
        shifted = summed - row_mean(summed)
        inv = lax.rsqrt(row_mean(shifted * shifted) + norm_eps)
        normed = shifted * inv
        down_in = (normed * dg_ref[...] + db_ref[...]).astype(BF16)
        ps_ref[tx] = mm(patch_sel, down_in, 1, 0)
        gp = gp_ref[tx]
        blocks = [gp[:, q * 256 : q * 256 + 256] for q in range(4)]
        scaled = [b * dg_ref[...] for b in blocks]
        centred = spread([s - row_mean(s) for s in scaled])
        second = row_mean(spread(scaled) * normed)
        grad_summed = inv * (centred - normed * second)
        for h in range(2):
            gs_ref[h, rows, :] = grad_summed[:, h * 128 : h * 128 + 128]
        add_entry(54, fold8(spread(blocks) * normed))
        add_entry(53, fold8(grad_summed * branch))
        scaled_grad = ls_ref[...] * grad_summed
        add_entry(52, fold8(scaled_grad))
        gb_ref[rows, :] = scaled_grad.astype(BF16)
        return c

    lax.fori_loop(0, 4, forward, 0)

    def batch(b):
        rings = ((yy, lambda k: {"sx": lax.rem(yy + k, 4) * 4 + lax.rem(sx, 4)}), (sy, lambda k: {"sy": at_sy(k)}))
        core_dev = {"sx": sx + 1 - 2 * core}
        x_dev = {"sx": sx + 2 - 4 * xl}

        def rc(src, dst, k, dev):
            return pltpu.make_async_remote_copy(
                src_ref=src, dst_ref=dst, send_sem=bs_sem.at[b, k], recv_sem=br_sem.at[b, k], device_id=dev,
                device_id_type=MESH,
            )

        def ds(i, n):
            return pl.ds(pl.multiple_of(i, n), n)

        fin = fin_ref.at[b]
        s0, r0, t0, r1 = s0_ref.at[b], r0_ref.at[b], t0_ref.at[b], r1_ref.at[b]
        t1, r2, t2, r3 = t1_ref.at[b], r2_ref.at[b], t2_ref.at[b], r3_ref.at[b]
        loc = loc_ref.at[b]

        def goff(half, depth):
            at = core * 1024 + half * 512
            if depth > 0:
                at = at + rings[half][0] * 128
            if depth > 1:
                at = at + rings[1 - half][0] * 32
            if depth > 2:
                at = at + xl * 16
            return at

        def core_in():
            return [rc(s0, r0, 0, core_dev)]

        def ring1_in():
            return [
                rc(t0.at[ds(half * 512 + lax.rem(rings[half][0] + k, 4) * 128, 128)],
                   r1.at[half * 3 + k - 1], 1 + half * 3 + k - 1, rings[half][1](k))
                for half in range(2) for k in range(1, 4)
            ]

        def ring2_in():
            return [
                rc(t1.at[half, ds(lax.rem(rings[1 - half][0] + k, 4) * 32, 32)],
                   r2.at[half * 3 + k - 1], 7 + half * 3 + k - 1, rings[1 - half][1](k))
                for half in range(2) for k in range(1, 4)
            ]

        def x_in():
            return [
                rc(t2.at[half, ds((1 - xl) * 16, 16)], r3.at[half], 13 + half, x_dev) for half in range(2)
            ]

        def x_out():
            return [
                rc(fin.at[ds(goff(half, 3), 16)], fin.at[ds(goff(half, 3), 16)], 15 + half, x_dev)
                for half in range(2)
            ]

        def ring2_out():
            return [
                rc(fin.at[ds(goff(half, 2), 32)], fin.at[ds(goff(half, 2), 32)], 17 + half * 3 + k - 1,
                   rings[1 - half][1](k))
                for half in range(2) for k in range(1, 4)
            ]

        def ring1_out():
            return [
                rc(fin.at[ds(goff(half, 1), 128)], fin.at[ds(goff(half, 1), 128)], 23 + half * 3 + k - 1,
                   rings[half][1](k))
                for half in range(2) for k in range(1, 4)
            ]

        def core_out():
            return [rc(fin.at[ds(core * 1024, 1024)], fin.at[ds(core * 1024, 1024)], 29, core_dev)]

        def start(copies):
            for copy in copies:
                copy.start()

        def wait(copies):
            for copy in copies:
                copy.wait()

        def step0():
            def cast(i, c):
                s0[ds(i * 128, 128), :] = loc[ds((1 - core) * 1024 + i * 128, 128), :].astype(BF16)
                return c

            lax.fori_loop(0, 8, cast, 0)
            start(core_in())

        def step1():
            wait(core_in())

            def add(i, c):
                t0[ds(i * 128, 128), :] = (
                    loc[ds(core * 1024 + i * 128, 128), :] + r0[ds(i * 128, 128), :].astype(F32)
                ).astype(BF16)
                return c

            lax.fori_loop(0, 8, add, 0)
            start(ring1_in())

        def step2():
            wait(ring1_in())
            for half in range(2):
                total = t0[ds(half * 512 + rings[half][0] * 128, 128), :].astype(F32)
                for k in range(3):
                    total = total + r1[half * 3 + k].astype(F32)
                t1[half] = total.astype(BF16)
            start(ring2_in())

        def step3():
            wait(ring2_in())
            for half in range(2):
                total = t1[half, ds(rings[1 - half][0] * 32, 32), :].astype(F32)
                for k in range(3):
                    total = total + r2[half * 3 + k].astype(F32)
                t2[half] = total.astype(BF16)
            start(x_in())

        def step4():
            wait(x_in())
            for half in range(2):
                total = t2[half, ds(xl * 16, 16), :].astype(F32) + r3[half].astype(F32)
                fin_ref[b, ds(goff(half, 3), 16), :] = total.astype(BF16)
            start(x_out())

        def step5():
            wait(x_out())
            start(ring2_out())

        def step6():
            wait(ring2_out())
            start(ring1_out())

        def step7():
            wait(ring1_out())
            start(core_out())

        def step8():
            wait(core_out())
            pltpu.make_async_copy(fin, big_ref.at[b], out_sem.at[b]).start()

        def step9():
            pltpu.make_async_copy(fin, big_ref.at[b], out_sem.at[b]).wait()

        return [step0, step1, step2, step3, step4, step5, step6, step7, step8, step9]

    first = batch(0)
    second = batch(1)

    gr = gr_ref[...]
    gr2 = jnp.concatenate([gr, gr], axis=0)
    pool = None
    for q in range(4):
        sums = ps_ref[:, q * 8 : q * 8 + 8, :].reshape(32, 256)
        high = sums.astype(BF16)
        low = (sums - high.astype(F32)).astype(BF16)
        both = jnp.concatenate([high, low], axis=0)
        grad_down = mm(both, gr2, 0, 0)
        loc_ref[0, q * 256 : q * 256 + 256, :] = grad_down[:, :256]
        loc_ref[0, 1024 + q * 256 : 1024 + q * 256 + 256, :] = grad_down[:, 256:]
        part = mm(both, dw_ref[q * 256 : q * 256 + 256, :], 1, 0)
        part = part[:32] + part[32:]
        pool = part if pool is None else pool + part
    tissue = jnp.concatenate([mv_ref[...].reshape(32, 128)] * 4, axis=1)
    pooled_ref[...] = (pool * (1.0 / 16.0) + do_ref[...]) * tissue
    first[0]()

    def backward(tx, c):
        rows = pl.ds(pl.multiple_of(tx * 256, 256), 256)
        grad_b = gb_ref[rows, :]
        normed_in = ni_ref[rows, :]
        grad_normed = None
        for j in range(4):
            cols = slice(j * 256, j * 256 + 256)
            grad_hidden = mm(grad_b, w2_ref[cols, :], 1, 1) * sl_ref[rows, cols]
            add_entry(56 + j, fold8(grad_hidden))
            grad_hidden_b = grad_hidden.astype(BF16)
            part = mm(grad_hidden_b, w1_ref[:, cols], 1, 1)
            grad_normed = part if grad_normed is None else grad_normed + part
            loc_ref[1, j * 256 : j * 256 + 256, :] += mm(normed_in, grad_hidden_b, 0, 0)
            loc_ref[1, 1024 + j * 256 : 1024 + j * 256 + 256, :] += mm(act_ref[rows, cols], grad_b, 0, 0)
        normed = nc_ref[rows, :]
        add_entry(50, fold8(grad_normed * normed))
        add_entry(51, fold8(grad_normed))
        scaled = grad_normed * ng_ref[...]
        inv = inv_ref[rows, :]
        inv = jnp.concatenate([inv, inv], axis=1)
        grad_conv = inv * (scaled - row_mean(scaled) - normed * row_mean(scaled * normed))
        add_entry(49, fold8(grad_conv))
        for h in range(2):
            half = grad_conv[:, h * 128 : h * 128 + 128]
            co_ref[h, rows, :] = half
            for x in range(8):
                for q in range(4):
                    at = (x * 4 + q) * 8
                    pg_ref[h, pl.ds((tx * 8 + x + 3) * PITCH + LEFT + q, 8, stride=4), :] = half[at : at + 8, :]

        @pl.when(tx == 0)
        def _():
            first[1]()

        @pl.when(tx == 2)
        def _():
            first[2]()

        return c

    lax.fori_loop(0, 4, backward, 0)
    first[3]()

    pack(1, pg_ref)
    for copy in halo_copies(1, pg_ref):
        copy.start()
    second[0]()

    def tap_step(i, c):
        h = i // 7
        a = lax.rem(i, 7)

        def rows_step(k, sums):
            sums = list(sums)
            for d in range(2):
                x = k * 2 + d
                rows = plane_rows(p_ref, h, x + a, 10)
                grads = [co_ref[h, block8(x * 4 + q), :] for q in range(4)]
                for b in range(7):
                    sums[b] = sums[b] + (
                        (rows[b] * grads[0] + rows[b + 1] * grads[1])
                        + (rows[b + 2] * grads[2] + rows[b + 3] * grads[3])
                    )
            return tuple(sums)

        sums = lax.fori_loop(0, WX // 2, rows_step, tuple(jnp.zeros((8, 128), F32) for _ in range(7)))
        for b in range(7):
            kg_ref[h, pl.ds(pl.multiple_of((a * 7 + b) * 8, 8), 8), :] = sums[b]

        @pl.when(i == 2)
        def _():
            first[4]()
            second[1]()

        @pl.when(i == 5)
        def _():
            first[5]()

        @pl.when(i == 8)
        def _():
            first[6]()

        @pl.when(i == 11)
        def _():
            second[2]()

        return c

    lax.fori_loop(0, 14, tap_step, 0)
    first[7]()

    for h in range(2):
        total = kg_ref[h, pl.ds(0, 64, stride=8), :]
        for s in range(1, 8):
            total = total + kg_ref[h, pl.ds(s, 64, stride=8), :]
        v_ref[h * 64 : h * 64 + 64, :] = total

    def small_rc(src, dst, k, dev):
        return pltpu.make_async_remote_copy(
            src_ref=src, dst_ref=dst, send_sem=vs_sem.at[k], recv_sem=vr_sem.at[k], device_id=dev,
            device_id_type=MESH,
        )

    def small_in(k):
        return small_rc(v_ref.at[block8(at_sx(k))], vr_ref.at[block8(sx)], k, {"sx": at_sx(k)})

    def small_z(k):
        return small_rc(vz_ref.at[sy], vz_ref.at[sy], 15 + k, {"sy": at_sy(k)})

    def small_out(k):
        return small_rc(vf_ref.at[block8(sx)], vf_ref.at[block8(sx)], 18 + k, {"sx": at_sx(k)})

    def each(make, act):
        def body(k, c):
            act(make(k))
            return c

        return body

    def small_step0():
        lax.fori_loop(1, N_SX, each(small_in, lambda copy: copy.start()), 0)
        vr_ref[block8(sx), :] = v_ref[block8(sx), :]

    def small_step1():
        lax.fori_loop(1, N_SX, each(small_in, lambda copy: copy.wait()), 0)
        vz_ref[sy] = jnp.sum(vr_ref[...].reshape(16, 8, 128), axis=0)
        for k in range(1, N_SY):
            small_z(k).start()

    def small_step2():
        for k in range(1, N_SY):
            small_z(k).wait()
        vf_ref[block8(sx), :] = (vz_ref[0] + vz_ref[1]) + (vz_ref[2] + vz_ref[3])
        lax.fori_loop(1, N_SX, each(small_out, lambda copy: copy.start()), 0)

    def small_step3():
        lax.fori_loop(1, N_SX, each(small_out, lambda copy: copy.wait()), 0)
        small_ref[...] = vf_ref[...]

    small_step0()

    for copy in halo_copies(1, pg_ref):
        copy.wait()
    unpack(1, pg_ref)

    def back_step(i, c):
        x = i * 2
        keep = mv_ref[x // 8]
        for h in range(2):
            sums = depthwise(pg_ref, h, x, True)
            for k in range(2):
                for q in range(4):
                    value = (sums[k][q] + gs_ref[h, block8((x + k) * 4 + q), :]) * keep
                    nat_ref[h, x + k, pl.ds(q, 8, stride=4), :] = value
        for k in range(2):
            gf_ref[x + k] = jnp.concatenate([nat_ref[0, x + k], nat_ref[1, x + k]], axis=1).astype(BF16)

        @pl.when(i == 3)
        def _():
            second[3]()
            small_step1()

        @pl.when(i == 7)
        def _():
            second[4]()
            small_step2()

        @pl.when(i == 9)
        def _():
            second[5]()

        @pl.when(i == 11)
        def _():
            second[6]()

        return c

    lax.fori_loop(0, WX // 2, back_step, 0)
    small_step3()
    second[7]()
    first[8]()
    second[8]()
    first[9]()
    second[9]()


def on_device(
    features,
    return_slot,
    returned_grads,
    conv_weight,
    conv_bias,
    norm_gain,
    norm_bias,
    expand_weight,
    expand_bias,
    project_weight,
    project_bias,
    layer_scale,
    down_gain,
    down_bias,
    down_weight,
    down_offset,
):
    vmem = pl.BlockSpec(memory_space=pltpu.VMEM)

    def row(v):
        return v.reshape(1, -1)

    def vm(*shape, dtype=F32):
        return pltpu.VMEM(shape, dtype)

    dma = pltpu.SemaphoreType.DMA
    pooled, grad_features, small, big = pl.pallas_call(
        kernel,
        out_shape=(
            jax.ShapeDtypeStruct((32, 512), F32),
            jax.ShapeDtypeStruct((WX, WY, 256), BF16),
            jax.ShapeDtypeStruct((128, 128), F32),
            jax.ShapeDtypeStruct((2, 2048, 256), BF16),
        ),
        in_specs=[pl.BlockSpec(memory_space=pltpu.SMEM)] + [vmem] * 15,
        out_specs=(vmem, vmem, vmem, pl.BlockSpec(memory_space=pl.ANY)),
        scratch_shapes=[
            vm(2, PLANE, 128), vm(2, PLANE, 128), vm(2, 2, 2, 3, 32, 128), vm(2, 2, 2, 3, 32, 128),
            vm(2, 4, 2, 3, 8, 128),
            vm(2, 49, 8, 128), vm(4, 32, 128), vm(4, 8, 128),
            vm(4, 32, 128), vm(128, 128), vm(128, 128), vm(4, 32, 128), vm(32, 512, dtype=BF16), vm(4, 8, 1024),
            vm(4, 32, 256),
            vm(2, 1024, 128), vm(1024, 256), vm(1024, 128), vm(1024, 256, dtype=BF16), vm(1024, 1024, dtype=BF16),
            vm(1024, 1024), vm(2, 1024, 128), vm(1024, 256, dtype=BF16), vm(2, 32, 32, 128),
            vm(2, 512, 128), vm(128, 128), vm(128, 128), vm(4, 8, 128), vm(128, 128),
            vm(2, 2048, 256), vm(2, 1024, 256, dtype=BF16), vm(2, 1024, 256, dtype=BF16),
            vm(2, 1024, 256, dtype=BF16), vm(2, 6, 128, 256, dtype=BF16), vm(2, 2, 128, 256, dtype=BF16),
            vm(2, 6, 32, 256, dtype=BF16), vm(2, 2, 32, 256, dtype=BF16), vm(2, 2, 16, 256, dtype=BF16),
            vm(2, 2048, 256, dtype=BF16),
            dma((2, 8)), dma((2, 8)), dma((16,)), dma((16,)), dma((2, 30)), dma((2, 30)), dma((34,)), dma((34,)),
            dma((2,)),
        ],
        compiler_params=pltpu.CompilerParams(
            collective_id=0, has_side_effects=True, vmem_limit_bytes=56 * 1024 * 1024
        ),
        cost_estimate=pl.CostEstimate(flops=4_000_000_000, bytes_accessed=8_000_000, transcendentals=1_000_000),
    )(
        return_slot, features, returned_grads[0], conv_weight, row(conv_bias), row(norm_gain), row(norm_bias),
        expand_weight, row(expand_bias), project_weight, row(project_bias), row(layer_scale), row(down_gain),
        row(down_bias), down_weight, row(down_offset),
    )
    pooled = pooled.reshape(4, 4, 2, 512)[:, :, 0].astype(BF16)
    down = jnp.concatenate([big[0, :1024], big[0, 1024:]], axis=1).astype(F32)
    expand = jnp.concatenate([big[1, j * 256 : j * 256 + 256] for j in range(4)], axis=1).astype(F32)
    project = big[1, 1024:].astype(F32)
    small = jnp.concatenate([small[:64], small[64:]], axis=1)
    return (
        pooled,
        grad_features,
        small[:49].reshape(7, 7, 256),
        expand,
        project,
        down,
        small[49:56],
        small[56:60].reshape(1024),
        small[60:62].reshape(512),
    )


def solution(mesh):
    placed = (
        P(("slide", "sx"), "sy", None),
        P(("slide", "sx"), "sy"),
        P("sy", ("slide", "sx"), None),
    ) + (P(),) * 13
    return jax.shard_map(
        on_device,
        mesh=mesh,
        in_specs=placed,
        out_specs=(
            P(("slide", "sx"), "sy", None),
            P(("slide", "sx"), "sy", None),
            P("slide", None, None),
            P("slide", None),
            P("slide", None),
            P("slide", None),
            P("slide", None),
            P("slide"),
            P("slide"),
        ),
        check_vma=False,
    )
```

time: 668 us -> 91.2 us (0.14)
  blocking collectives: 272 us -> 0 us
  waiting for transfers between devices: 249 us -> 0 us
  Pallas kernels: 0 us -> 78.4 us
  other arithmetic: 46.6 us -> 6.64 us
  local copies, waits for them, and re-layouts: 36.9 us -> 5.15 us
  starting transfers between devices: 26.7 us -> 0 us
  matrix products: 18.1 us -> 0 us
  between operations: 15.4 us -> 0.67 us
    psum x1 -> x0, blocking collectives: 272 us -> none  [on_device(): lax.psum((grad_down_weight, grad_down_offset, grad_down_gain, grad_down_b...]
    psum x1 -> x0, waiting for transfers between devices: 244 us -> none  [on_device(): lax.psum((grad_down_weight, grad_down_offset, grad_down_gain, grad_down_b...]
    pallas_call x0 -> x1, Pallas kernels: none -> 78.4 us  [on_device(): pl.pallas_call(kernel, out_shape=(jax.ShapeDtypeStruct((32, 512), F32), j...]
    reduce_sum x13 -> x0, other arithmetic: 27.6 us -> none  [the longest x3 10.5 us: kernel_grad(): cols_list.append(jnp.sum(window * grad_out, axis=(0, 1)))]
    ppermute x8 -> x0, starting transfers between devices: 20.6 us -> none  [the longest x4 14.1 us: with_halo(): before = lax.ppermute(last, axis, up)]
    dot_general x10 -> x0, matrix products: 18.1 us -> none  [the longest x1 3.81 us: on_device(): lax.dot_general(grad_branch_b, project_weight, (((1,), (1,)), ((), ())),...]
    convert_element_type x7 -> x2, other arithmetic: 15.8 us -> 2.7 us  [the longest x1 1.61 us: on_device(): down = jnp.concatenate([big[0, :1024], big[0, 1024:]], axis=1).astype(F32)]
    unnamed x185 -> x6, local copies, waits for them, and re-layouts: 15.5 us -> 2.59 us
  transfers between devices with their start and end apart: 10 -> 0, of which waited for: 3 -> 0; matrix products, arithmetic and copies ran while one was open for 7% -> 0% of each run, Pallas kernels for 0% -> 0%
where the time goes in v1:
time: 91.2 us; the launch traced here: 90.9 us
  Pallas kernels  78.4 us (86%)
  other arithmetic  6.64 us (7%)
  local copies, waits for them, and re-layouts  5.15 us (6%)
    pallas_call x1, Pallas kernels, on_device(): pl.pallas_call(kernel, out_shape=(jax.ShapeDtypeStruct((32, 512), F32), j...  78.4 us
    unnamed x6, local copies, waits for them, and re-layouts  2.59 us
    squeeze x1, other arithmetic, on_device(): down = jnp.concatenate([big[0, :1024], big[0, 1024:]], axis=1).astype(F32)  2.48 us

profile of v1, /device:TPU:1, one launch (start us, length us, event | category | flops | bytes accessed | tf_op | source)
XLA Modules:
  0.0 90.9 jit_solution(12210045851642670546)
XLA Ops:
  0.6 78.4 %shard_map.223 = (f32[32,512]{1,0:T(8,128)}, bf16[32,32,256]{2,1,0:T(8,128)(2,1)}, f32[128,128]{1,0:T(8,128)}, bf16[2,2048,256]{2,1,0:T(8,128)(2,1)}) custom-call(s32[4,4]{1,0:T(4,128)} %slot_ref.1, bf16[32,32,256]{2,1,0:T(8,128)(2,1)} %feat_ref.1, bf16[32,512]{1,0:T(8,128)(2,1)} %bitcast.39, f32[7,7,256]{2,1,0:T(8,128)} %cw_ref.1, f32[1,256]{1,0:T(1,128)} %bitcast.42, ...), custom_call_target="tpu_custom_call" | custom-call | flops 4000000000 | bytes 8000000 | tf_op jit(solution)/shard_map/pallas_call | solution.py:716
  79.1 0.8 convert.5
  79.9 0.6 copy.30
  80.6 0.8 fusion.5
  81.3 0.6 copy.28
  81.9 0.6 copy.27
  82.5 0.6 fusion.1
  83.1 0.6 reshape.71
  83.8 1.1 %slice_bitcast_fusion.5 = (bf16[256,256]{1,0:T(8,128)(2,1)S(1)}, bf16[256,256]{1,0:T(8,128)(2,1)S(1)}, bf16[256,256]{1,0:T(8,128)(2,1)S(1)}, bf16[256,256]{1,0:T(8,128)(2,1)S(1)}) fusion(bf16[2,2048,256]{2,1,0:T(8,128)(2,1)} %get-tuple-element.16), kind=kLoop, calls=%fused_computation.8 | loop fusion | bytes 1048576 | tf_op jit(solution)/shard_map/squeeze | solution.py:753
  84.9 2.5 %slice_bitcast_fusion.1 = (bf16[1024,256]{1,0:T(8,128)(2,1)S(1)}, bf16[1024,256]{1,0:T(8,128)(2,1)S(1)}, f32[1024,256]{1,0:T(8,128)}) fusion(bf16[2,2048,256]{2,1,0:T(8,128)(2,1)} %get-tuple-element.16), kind=kLoop, calls=%fused_computation.4 | loop fusion | flops 262144 | bytes 3670016 | tf_op jit(solution)/shard_map/squeeze | solution.py:752
  87.4 0.0 copy-start
  87.4 1.1 %maximum_convert_fusion.1 = f32[256,1024]{1,0:T(8,128)} fusion(bf16[256,256]{1,0:T(8,128)(2,1)S(1)} %get-tuple-element.21, bf16[256,256]{1,0:T(8,128)(2,1)S(1)} %get-tuple-element.22, bf16[256,256]{1,0:T(8,128)(2,1)S(1)} %get-tuple-element.23, bf16[256,256]{1,0:T(8,128)(2,1)S(1)} %get-tuple-element.20), kind=kLoop, calls=%fused_computation.1 | loop fusion | flops 2097152 | bytes 1572864 | tf_op jit(solution)/shard_map/convert_element_type | solution.py:753
  88.5 1.6 %maximum_convert_fusion = f32[1024,512]{1,0:T(8,128)} fusion(bf16[1024,256]{1,0:T(8,128)(2,1)S(1)} %get-tuple-element.18, bf16[1024,256]{1,0:T(8,128)(2,1)S(1)} %get-tuple-element.17), kind=kLoop, calls=%fused_computation | loop fusion | flops 2097152 | bytes 3145728 | tf_op jit(solution)/shard_map/convert_element_type | solution.py:752
  90.1 0.0 copy-done
  90.1 0.8 copy.32
  (4 shorter events, 0.0 us)
Async XLA Ops:
  87.4 2.7 %copy-start = (bf16[32,32,256]{2,1,0:T(8,128)(2,1)S(1)}, bf16[32,32,256]{2,1,0:T(8,128)(2,1)}, u32[]{:S(2)}) copy-start(bf16[32,32,256]{2,1,0:T(8,128)(2,1)} %get-tuple-element.36) | copy-start | bytes 1572868

commit v2 on v1

v2 whole, which is shorter than its diff:
```python
import functools

import jax
import jax.numpy as jnp
from jax import lax
from jax.experimental import pallas as pl
from jax.experimental.pallas import tpu as pltpu
from jax.sharding import PartitionSpec as P

F32 = jnp.float32
BF16 = jnp.bfloat16
MESH = pl.DeviceIdType.MESH

norm_eps = 1e-06
gelu_scale = 0.7978845608028654
gelu_cubic = 0.044715

WX = 32
WY = 32
LEFT = 8
PITCH = 48
PLANE = 38 * PITCH
N_SX = 16
N_SY = 4


def mm(a, b, ca, cb):
    return lax.dot_general(a, b, (((ca,), (cb,)), ((), ())), preferred_element_type=F32)


def fold8(v):
    return jnp.sum(v.reshape(v.shape[0] // 8, 8, v.shape[1]), axis=0)


def row_mean(v):
    return jnp.sum(v, axis=-1, keepdims=True) * (1.0 / v.shape[-1])


def kernel(
    slot_hbm, feat_hbm, ret_hbm, cw_hbm, cb_hbm, ng_hbm, nb_hbm, w1_hbm, b1_hbm, w2_hbm, b2_hbm, ls_hbm, dg_hbm,
    db_hbm, dw_hbm, do_hbm,
    pooled_hbm, gf_hbm, small_hbm, expand_ref, project_ref, down_ref,
    slot_ref, feat_ref, ret_ref, cw_ref, cb_ref, ng_ref, nb_ref, w1_ref, b1_ref, w2_ref, b2_ref, ls_ref, dg_ref,
    db_ref, dw_ref, do_ref, pooled_ref, gf_ref, small_ref, in_sem, res_sem,
    p_ref, pg_ref, xp_ref, xr_ref, yp_ref, yr_ref, cr_ref, wb_ref, mn_ref, mv_ref,
    rg_ref, pk_ref, rv_ref, ar_ref, gr_ref, gp_ref, ps_ref,
    co_ref, nc_ref, inv_ref, nit_ref, gbt_ref, gh_ref, act_ref, sl_ref, gs_ref, gb_ref, nat_ref,
    kg_ref, v_ref, vr_ref, vz_ref, vf_ref,
    loc_ref, s0_ref, r0_ref, s1_ref, r1_ref, s2_ref, r2_ref, fin_ref,
    hs_sem, hr_sem, as_sem, ar_sem, bs_sem, br_sem, vs_sem, vr_sem, out_sem,
):
    pairs = (
        (slot_hbm, slot_ref), (feat_hbm, feat_ref), (ret_hbm, ret_ref), (cw_hbm, cw_ref), (cb_hbm, cb_ref),
        (dw_hbm, dw_ref), (w1_hbm, w1_ref), (w2_hbm, w2_ref), (ng_hbm, ng_ref), (nb_hbm, nb_ref), (b1_hbm, b1_ref),
        (b2_hbm, b2_ref), (ls_hbm, ls_ref), (dg_hbm, dg_ref), (db_hbm, db_ref), (do_hbm, do_ref),
    )
    loads = [pltpu.make_async_copy(src, dst, in_sem.at[k]) for k, (src, dst) in enumerate(pairs)]
    for load in loads:
        load.start()

    sx = lax.axis_index("sx")
    sy = lax.axis_index("sy")
    core = lax.rem(sx, 2)
    xl = lax.rem(sx // 2, 2)
    yy = sx // 4

    def at_sx(k):
        return lax.rem(sx + k + N_SX, N_SX)

    def at_sy(k):
        return lax.rem(sy + k + N_SY, N_SY)

    barrier = pltpu.get_barrier_semaphore()

    def greet(k, c):
        pl.semaphore_signal(barrier, inc=1, device_id={"sx": at_sx(k)}, device_id_type=MESH)
        return c

    lax.fori_loop(1, N_SX, greet, 0)
    for k in range(1, N_SY):
        pl.semaphore_signal(barrier, inc=1, device_id={"sy": at_sy(k)}, device_id_type=MESH)
    for k in range(1, N_SY):
        pl.semaphore_signal(
            barrier, inc=1, device_id={"sx": sx + 2 - 4 * xl, "sy": at_sy(k)}, device_id_type=MESH
        )
    for i in (-1, 1):
        for j in (-1, 1):
            pl.semaphore_signal(barrier, inc=1, device_id={"sx": at_sx(i), "sy": at_sy(j)}, device_id_type=MESH)

    loads[0].wait()
    sub = lax.broadcasted_iota(jnp.int32, (8, 128), 0)
    lane = lax.broadcasted_iota(jnp.int32, (8, 128), 1)
    sel = []
    for tx in range(4):
        picked = jnp.zeros((8, 128), jnp.int32)
        for ty in range(4):
            s = slot_ref[tx, ty]
            picked = jnp.where(sub // 2 == ty, s, picked)
            mn_ref[tx, ty * 8 : ty * 8 + 8, :] = jnp.where(jnp.full((8, 128), s) >= 0, 1.0, 0.0).astype(F32)
        mv_ref[tx] = jnp.where(picked >= 0, 1.0, 0.0).astype(F32)
        sel.append(jnp.where(picked == lane, 1.0, 0.0).astype(F32))
    selector = jnp.concatenate(sel, axis=0).astype(BF16)[:, :32]

    loads[1].wait()
    def fill(x, c):
        f = feat_ref[x].astype(F32)
        m = mn_ref[x // 8]
        at = pl.multiple_of((x + 3) * PITCH + LEFT, 8)
        for h in range(2):
            p_ref[h, pl.ds(at, WY), :] = f[:, h * 128 : h * 128 + 128] * m
            p_ref[h, pl.ds(at - 8, 8), :] = jnp.zeros((8, 128), F32)
            p_ref[h, pl.ds(at + WY, 8), :] = jnp.zeros((8, 128), F32)
        return c

    lax.fori_loop(0, WX, fill, 0)
    for row in (0, 35):
        p_ref[:, row * PITCH : (row + 3) * PITCH, :] = jnp.zeros((2, 3 * PITCH, 128), F32)

    def pack(e, ref):
        for side, row in ((0, 3), (1, 32)):
            for h in range(2):
                for a in range(3):
                    xp_ref[e, side, h, a] = ref[
                        h, pl.ds((row + a) * PITCH + LEFT, WY), :
                    ].astype(BF16)
        for side, col in ((0, 0), (1, WY - 3)):
            for h in range(2):
                for c in range(3):
                    yp_ref[e, side, h, c] = ref[h, pl.ds(3 * PITCH + LEFT + col + c, WX, stride=PITCH), :].astype(BF16)

    def halo_copies(e):
        def rc(src, dst, k, dev):
            return pltpu.make_async_remote_copy(
                src_ref=src, dst_ref=dst, send_sem=hs_sem.at[e, k], recv_sem=hr_sem.at[e, k], device_id=dev,
                device_id_type=MESH,
            )

        out = []
        for side, step in ((0, -1), (1, 1)):
            out.append(rc(yp_ref.at[e, side], yr_ref.at[e, side], 2 + side, {"sy": at_sy(step)}))
            out.append(rc(xp_ref.at[e, side], xr_ref.at[e, side], side, {"sx": at_sx(step)}))
            out.append(
                rc(yp_ref.at[e, side, :, :, 16:32, :], cr_ref.at[e, 2 * side], 4 + 2 * side,
                   {"sx": at_sx(1), "sy": at_sy(step)})
            )
            out.append(
                rc(yp_ref.at[e, side, :, :, 0:16, :], cr_ref.at[e, 2 * side + 1], 5 + 2 * side,
                   {"sx": at_sx(-1), "sy": at_sy(step)})
            )
        return out

    has_top = sx > 0
    has_bottom = sx < N_SX - 1
    keep_below = jnp.where(has_bottom, 1.0, 0.0).astype(F32)
    keep_above = jnp.where(has_top, 1.0, 0.0).astype(F32)
    keep_right = jnp.where(sy < N_SY - 1, 1.0, 0.0).astype(F32)
    keep_left = jnp.where(sy > 0, 1.0, 0.0).astype(F32)

    def unpack_sides(e, ref):
        for side, col, keep in ((0, LEFT + WY, keep_right), (1, LEFT - 3, keep_left)):
            for h in range(2):
                for c in range(3):
                    ref[h, pl.ds(3 * PITCH + col + c, WX, stride=PITCH), :] = (
                        yr_ref[e, side, h, c].astype(F32) * keep
                    )

    def unpack_ends(e, ref):
        for side, row, keep in ((0, 35, keep_below), (1, 0, keep_above)):
            for h in range(2):
                for a in range(3):
                    ref[h, pl.ds((row + a) * PITCH + LEFT, WY), :] = xr_ref[e, side, h, a].astype(F32) * keep
        for side, col, keep in ((0, LEFT + WY, keep_right), (1, LEFT - 3, keep_left)):
            for h in range(2):
                for c in range(3):
                    top = cr_ref[e, 2 * side, h, c].astype(F32) * (keep * keep_above)
                    ref[h, pl.ds(col + c, 3, stride=PITCH), :] = top[13:16, :]
                    bottom = cr_ref[e, 2 * side + 1, h, c].astype(F32) * (keep * keep_below)
                    ref[h, pl.ds(35 * PITCH + col + c, 3, stride=PITCH), :] = bottom[0:3, :]

    pack(0, p_ref)

    loads[2].wait()
    for q in range(4):
        rg_ref[q] = ret_ref[:, q * 128 : q * 128 + 128].astype(F32)
    for q in range(4):
        for s in range(2):
            pk_ref[pl.ds(2 * q + s, 16, stride=8), :] = rg_ref[q, pl.ds(s, 16, stride=2), :]

    pl.semaphore_wait(barrier, (N_SX - 1) + 2 * (N_SY - 1) + 4)

    for copy in halo_copies(0):
        copy.start()

    def block8(i):
        return pl.ds(pl.multiple_of(i * 8, 8), 8)

    def return_copy(k):
        return pltpu.make_async_remote_copy(
            src_ref=pk_ref.at[block8(at_sx(k))], dst_ref=rv_ref.at[block8(sx)], send_sem=as_sem.at[k],
            recv_sem=ar_sem.at[k], device_id={"sx": at_sx(k)}, device_id_type=MESH,
        )

    def start_return(k, c):
        return_copy(k).start()
        return c

    lax.fori_loop(1, N_SX, start_return, 0)
    rv_ref[block8(sx), :] = pk_ref[block8(sx), :]

    loads[3].wait()
    for h in range(2):
        for a in range(7):
            for b in range(7):
                wb_ref[h, a * 7 + b] = jnp.broadcast_to(cw_ref[a, b : b + 1, h * 128 : h * 128 + 128], (8, 128))

    kg_ref[...] = jnp.zeros_like(kg_ref)

    def add_entry(t, value):
        for h in range(2):
            kg_ref[h, t * 8 : t * 8 + 8, :] += value[:, h * 128 : h * 128 + 128]

    def plane_rows(ref, h, x, n):
        return [ref[h, pl.ds(x * PITCH + (LEFT - 3) + c, 8, stride=4), :] for c in range(n)]

    def depthwise(ref, h, x, flipped):
        sums = [[None] * 4 for _ in range(2)]
        for r in range(8):
            rows = plane_rows(ref, h, x + r, 10)
            for i in range(2):
                a = r - i
                if a < 0 or a > 6:
                    continue
                for b in range(7):
                    t = a * 7 + b
                    w = wb_ref[h, 48 - t if flipped else t]
                    for c in range(4):
                        term = rows[c + b] * w
                        sums[i][c] = term if sums[i][c] is None else sums[i][c] + term
        return sums

    loads[4].wait()

    def conv_step(i, c):
        x = i * 2
        for h in range(2):
            bias = cb_ref[:, h * 128 : h * 128 + 128]
            sums = depthwise(p_ref, h, x, False)
            for k in range(2):
                for q in range(4):
                    co_ref[h, block8((x + k) * 4 + q), :] = sums[k][q] + bias
        return c

    lax.fori_loop(0, WX // 2, conv_step, 0)

    loads[5].wait()

    def wait_return(k, c):
        return_copy(k).wait()
        return c

    lax.fori_loop(1, N_SX, wait_return, 0)
    for q in range(4):
        for s in range(2):
            ar_ref[q, pl.ds(s, 16, stride=2), :] = rv_ref[pl.ds(2 * q + s, 16, stride=8), :]
    arrived = jnp.concatenate([ar_ref[q] for q in range(4)], axis=1).astype(BF16)
    grad_pool = mm(selector, arrived, 1, 0)
    grad_reduced = (grad_pool * (1.0 / 16.0)).astype(BF16)
    gr_ref[...] = grad_reduced
    grad_patch = mm(grad_reduced, dw_ref[...], 1, 1)
    for tx in range(4):
        gp_ref[tx] = grad_patch[tx * 8 : tx * 8 + 8, :]

    off_sum = jnp.sum(grad_pool.reshape(4, 8, 512), axis=0) * 0.5
    for q in range(2):
        add_entry(60 + q, off_sum[:, q * 256 : q * 256 + 256])
    bias_sum = jnp.sum(gp_ref[...], axis=0)
    bias_sum = (
        bias_sum[:, 0:256] + bias_sum[:, 256:512] + bias_sum[:, 512:768] + bias_sum[:, 768:1024]
    ) * 8.0
    add_entry(55, bias_sum)

    for copy in halo_copies(0):
        copy.wait()
    unpack_sides(0, p_ref)

    def side_step(g, c):
        for h in range(2):
            for first_col, taps_of, out_y in (
                (LEFT - 3, ((0, 0, 0), (0, 1, 1), (0, 2, 2), (1, 0, 1), (1, 1, 2), (2, 0, 2)), 0),
                (LEFT + WY, ((0, 6, 0), (1, 5, 0), (1, 6, 1), (2, 4, 0), (2, 5, 1), (2, 6, 2)), 29),
            ):
                sums = [None] * 3
                for a in range(7):
                    cols = [p_ref[h, pl.ds((g * 8 + a) * PITCH + first_col + q, 8, stride=PITCH), :] for q in range(3)]
                    for y, b, q in taps_of:
                        term = cols[q] * wb_ref[h, a * 7 + b]
                        sums[y] = term if sums[y] is None else sums[y] + term
                for y in range(3):
                    row = (out_y + y) % 4 * 8 + (out_y + y) // 4
                    at = pl.ds(g * 256 + row, 8, stride=32)
                    co_ref[h, at, :] = co_ref[h, at, :] + sums[y]
        return c

    lax.fori_loop(0, 4, side_step, 0)
    unpack_ends(0, p_ref)

    def end_step(h, c):
        for first_row, pairs_of in (
            (0, ((0, 0), (0, 1), (0, 2), (1, 0), (1, 1), (2, 0))),
            (29, ((0, 6), (1, 5), (1, 6), (2, 4), (2, 5), (2, 6))),
        ):
            sums = [[None] * 4 for _ in range(3)]
            for x, a in pairs_of:
                rows = plane_rows(p_ref, h, first_row + x + a, 10)
                for b in range(7):
                    w = wb_ref[h, a * 7 + b]
                    for q in range(4):
                        term = rows[q + b] * w
                        sums[x][q] = term if sums[x][q] is None else sums[x][q] + term
            for x in range(3):
                for q in range(4):
                    row = ((first_row + x) * 4 + q) * 8
                    co_ref[h, row : row + 8, :] = co_ref[h, row : row + 8, :] + sums[x][q]
        return c

    lax.fori_loop(0, 2, end_step, 0)

    for load in loads[6:]:
        load.wait()
    r32 = lax.broadcasted_iota(jnp.int32, (32, 256), 0)
    k32 = lax.broadcasted_iota(jnp.int32, (32, 256), 1)
    off_of = (k32 // 32 % 2) * 2 + (k32 // 8 % 4) % 2
    patch_sel = jnp.where(
        (off_of == r32 // 8) & (k32 % 8 // 2 == r32 % 8 // 2) & (r32 % 2 == 0), 1.0, 0.0
    ).astype(BF16)

    def spread(blocks):
        row = [blocks[0], blocks[1]] * 2 + [blocks[2], blocks[3]] * 2
        return jnp.concatenate(row * 4, axis=0)

    def forward(tx, c):
        rows = pl.ds(pl.multiple_of(tx * 256, 256), 256)
        v = jnp.concatenate([co_ref[0, rows, :], co_ref[1, rows, :]], axis=1)
        shifted = v - row_mean(v)
        inv = lax.rsqrt(row_mean(shifted * shifted) + norm_eps)
        normed = shifted * inv
        nc_ref[rows, :] = normed
        inv_ref[rows, :] = jnp.broadcast_to(inv, (256, 128))
        normed_in = (normed * ng_ref[...] + nb_ref[...]).astype(BF16)
        branch = None
        for j in range(4):
            cols = slice(j * 256, j * 256 + 256)
            hid = mm(normed_in, w1_ref[:, cols], 1, 0) + b1_ref[:, cols]
            sq = hid * hid
            t = jnp.tanh(hid * (gelu_scale + (gelu_scale * gelu_cubic) * sq))
            u = 0.5 + 0.5 * t
            act = (hid * u).astype(BF16)
            act_ref[rows, cols] = act
            sl_ref[rows, cols] = u + hid * (u - u * t) * (gelu_scale + (3.0 * gelu_scale * gelu_cubic) * sq)
            part = mm(act, w2_ref[cols, :], 1, 0)
            branch = part if branch is None else branch + part
        branch = branch + b2_ref[...]
        masked = jnp.concatenate(
            [
                jnp.concatenate(
                    [
                        p_ref[h, pl.ds((tx * 8 + x + 3) * PITCH + LEFT + q, 8, stride=4), :]
                        for x in range(8)
                        for q in range(4)
                    ],
                    axis=0,
                )
                for h in range(2)
            ],
            axis=1,
        )
        summed = (masked + ls_ref[...] * branch).astype(BF16).astype(F32)
        shifted = summed - row_mean(summed)
        inv = lax.rsqrt(row_mean(shifted * shifted) + norm_eps)
        normed = shifted * inv
        down_in = (normed * dg_ref[...] + db_ref[...]).astype(BF16)
        ps_ref[tx] = mm(patch_sel, down_in, 1, 0)
        gp = gp_ref[tx]
        blocks = [gp[:, q * 256 : q * 256 + 256] for q in range(4)]
        scaled = [b * dg_ref[...] for b in blocks]
        centred = spread([s - row_mean(s) for s in scaled])
        second = row_mean(spread(scaled) * normed)
        grad_summed = inv * (centred - normed * second)
        for h in range(2):
            gs_ref[h, rows, :] = grad_summed[:, h * 128 : h * 128 + 128]
        add_entry(54, fold8(spread(blocks) * normed))
        add_entry(53, fold8(grad_summed * branch))
        scaled_grad = ls_ref[...] * grad_summed
        add_entry(52, fold8(scaled_grad))
        grad_b = scaled_grad.astype(BF16)
        gb_ref[rows, :] = grad_b
        gbt_ref[:, rows] = grad_b.T
        nit_ref[:, rows] = normed_in.T
        return c

    lax.fori_loop(0, 4, forward, 0)

    def batch(b):
        core_dev = {"sx": sx + 1 - 2 * core}

        def y_dev(k, m):
            x_core = lax.rem(sx, 4) if m == 0 else lax.rem(sx + 2, 4)
            return {"sx": lax.rem(yy + k, 4) * 4 + x_core}

        def z_dev(k, m):
            return {"sy": at_sy(k)} if m == 0 else {"sy": at_sy(k), "sx": sx + 2 - 4 * xl}

        rings = ((yy, y_dev), (sy, z_dev))
        others = [(k, m) for m in range(2) for k in range(4) if (k, m) != (0, 0)]

        def rc(src, dst, k, dev):
            return pltpu.make_async_remote_copy(
                src_ref=src, dst_ref=dst, send_sem=bs_sem.at[b, k], recv_sem=br_sem.at[b, k], device_id=dev,
                device_id_type=MESH,
            )

        def ds(i, n):
            return pl.ds(pl.multiple_of(i, n), n)

        fin = fin_ref.at[b]
        loc = loc_ref.at[b]
        s0, r0, r1 = s0_ref.at[b], r0_ref.at[b], r1_ref.at[b]
        s1, s2, r2 = s1_ref.at[b], s2_ref.at[b], r2_ref.at[b]

        def ring_at(half, k=0):
            return half * 512 + lax.rem(rings[half][0] + k, 4) * 128

        def plane_at(half, k=0, m=0):
            return lax.rem(rings[1 - half][0] + k, 4) * 32 + (xl if m == 0 else 1 - xl) * 16

        def core_in(q):
            return rc(s0.at[ds(q * 256, 256)], r0.at[ds(q * 256, 256)], q, core_dev)

        def ring_in(half, k):
            return rc(s1.at[ds(ring_at(half, k), 128)], r1.at[half, k - 1], 4 + half * 3 + k - 1, rings[half][1](k, 0))

        def plane_in(half, i):
            k, m = others[i]
            return rc(
                s2.at[half, ds(plane_at(half, k, m), 16)], r2.at[half, i], 10 + half * 7 + i, rings[1 - half][1](k, m)
            )

        def plane_out(half, i):
            k, m = others[i]
            at = ds(core * 1024 + ring_at(half) + plane_at(half), 16)
            return rc(fin.at[at], fin.at[at], 24 + half * 7 + i, rings[1 - half][1](k, m))

        def ring_out(half, k):
            at = ds(core * 1024 + ring_at(half), 128)
            return rc(fin.at[at], fin.at[at], 38 + half * 3 + k - 1, rings[half][1](k, 0))

        def core_out(half, k):
            at = ds(core * 1024 + ring_at(half, (4 - k) % 4), 128)
            return rc(fin.at[at], fin.at[at], 44 + half * 4 + k, core_dev)

        def step0(part=None):
            for q in range(4) if part is None else part:
                s0[ds(q * 256, 256), :] = loc[ds((1 - core) * 1024 + q * 256, 256), :].astype(BF16)
                core_in(q).start()

        def step1():
            for half in range(2):
                for q in (2 * half, 2 * half + 1):
                    core_in(q).wait()
                    at = ds(core * 1024 + q * 256, 256)
                    total = loc[at, :] + r0[ds(q * 256, 256), :].astype(F32)
                    loc[at, :] = total
                    s1[ds(q * 256, 256), :] = total.astype(BF16)
                for k in (2, 1, 3):
                    ring_in(half, k).start()

        def step2():
            for half in range(2):
                total = loc[ds(core * 1024 + ring_at(half), 128), :]
                for k in range(1, 4):
                    ring_in(half, k).wait()
                    total = total + r1[half, k - 1].astype(F32)
                loc[ds(core * 1024 + ring_at(half), 128), :] = total
                s2[half] = total.astype(BF16)
                for i in range(7):
                    plane_in(half, i).start()

        def step3():
            for half in range(2):
                at = ds(core * 1024 + ring_at(half) + plane_at(half), 16)
                total = loc[at, :]
                for i in range(7):
                    plane_in(half, i).wait()
                    total = total + r2[half, i].astype(F32)
                fin[at, :] = total.astype(BF16)
                for i in range(7):
                    plane_out(half, i).start()

        def step4():
            for half in range(2):
                for i in range(7):
                    plane_out(half, i).wait()
                for k in (2, 1, 3):
                    ring_out(half, k).start()
                core_out(half, 0).start()

        def step5():
            for half in range(2):
                for k in (1, 3, 2):
                    ring_out(half, k).wait()
                    core_out(half, k).start()

        def out_copies():
            if b == 0:
                return [
                    pltpu.make_async_copy(
                        fin.at[pl.ds(q * 1024, 1024)], down_ref.at[:, q * 256 : q * 256 + 256], out_sem.at[b, q]
                    )
                    for q in range(2)
                ]
            return [
                pltpu.make_async_copy(
                    fin.at[pl.ds(q * 256, 256)], expand_ref.at[:, q * 256 : q * 256 + 256], out_sem.at[b, q]
                )
                for q in range(4)
            ] + [pltpu.make_async_copy(fin.at[pl.ds(1024, 1024)], project_ref, out_sem.at[b, 4])]

        def step6():
            for half in range(2):
                for k in range(4):
                    core_out(half, k).wait()
            for copy in out_copies():
                copy.start()

        def step7():
            for copy in out_copies():
                copy.wait()

        return [step0, step1, step2, step3, step4, step5, step6, step7]

    first = batch(0)
    second = batch(1)

    gr = gr_ref[...]
    gr2 = jnp.concatenate([gr, gr], axis=0)
    pool = None
    for q in range(4):
        sums = ps_ref[:, q * 8 : q * 8 + 8, :].reshape(32, 256)
        high = sums.astype(BF16)
        low = (sums - high.astype(F32)).astype(BF16)
        both = jnp.concatenate([high, low], axis=0)
        grad_down = mm(both, gr2, 0, 0)
        loc_ref[0, q * 256 : q * 256 + 256, :] = grad_down[:, :256]
        loc_ref[0, 1024 + q * 256 : 1024 + q * 256 + 256, :] = grad_down[:, 256:]
        part = mm(both, dw_ref[q * 256 : q * 256 + 256, :], 1, 0)
        part = part[:32] + part[32:]
        pool = part if pool is None else pool + part
    tissue = jnp.concatenate([mv_ref[...].reshape(32, 128)] * 4, axis=1)
    pooled_ref[...] = (pool * (1.0 / 16.0) + do_ref[...]) * tissue
    pooled_out = pltpu.make_async_copy(pooled_ref, pooled_hbm, res_sem.at[0])
    pooled_out.start()
    first[0]()

    def hidden_back(j):
        cols = slice(j * 256, j * 256 + 256)
        grad_hidden = mm(gb_ref[...], w2_ref[cols, :], 1, 1) * sl_ref[:, cols]
        add_entry(56 + j, fold8(grad_hidden))
        grad_hidden_b = grad_hidden.astype(BF16)
        gh_ref[:, cols] = grad_hidden_b
        loc_ref[1, j * 256 : j * 256 + 256, :] = mm(nit_ref[...], grad_hidden_b, 1, 0)
        loc_ref[1, 1024 + j * 256 : 1024 + j * 256 + 256, :] = mm(gbt_ref[...], act_ref[:, cols], 1, 0).T

    hidden_back(0)
    hidden_back(1)
    first[1]()
    hidden_back(2)
    hidden_back(3)
    second[0]()

    def backward(tx, c):
        rows = pl.ds(pl.multiple_of(tx * 256, 256), 256)
        grad_normed = mm(gh_ref[rows, :], w1_ref[...], 1, 1)
        normed = nc_ref[rows, :]
        add_entry(50, fold8(grad_normed * normed))
        add_entry(51, fold8(grad_normed))
        scaled = grad_normed * ng_ref[...]
        inv = inv_ref[rows, :]
        inv = jnp.concatenate([inv, inv], axis=1)
        grad_conv = inv * (scaled - row_mean(scaled) - normed * row_mean(scaled * normed))
        add_entry(49, fold8(grad_conv))
        for h in range(2):
            half = grad_conv[:, h * 128 : h * 128 + 128]
            co_ref[h, rows, :] = half
            for x in range(8):
                for q in range(4):
                    at = (x * 4 + q) * 8
                    pg_ref[h, pl.ds((tx * 8 + x + 3) * PITCH + LEFT + q, 8, stride=4), :] = half[at : at + 8, :]

        @pl.when(tx == 1)
        def _():
            second[1]()

        return c

    lax.fori_loop(0, 4, backward, 0)

    pack(1, pg_ref)
    for copy in halo_copies(1):
        copy.start()

    def taps(a0, n, hooks):
        def half_step(h, c):
            def rows_step(i, sums):
                x = i * 2
                sums = list(sums)
                grads = [[co_ref[h, block8((x + d) * 4 + q), :] for q in range(4)] for d in range(2)]
                for r in range(n + 1):
                    rows = plane_rows(p_ref, h, x + a0 + r, 10)
                    for d in range(2):
                        a = r - d
                        if a < 0 or a >= n:
                            continue
                        for b in range(7):
                            g = grads[d]
                            sums[a * 7 + b] = sums[a * 7 + b] + (
                                (rows[b] * g[0] + rows[b + 1] * g[1]) + (rows[b + 2] * g[2] + rows[b + 3] * g[3])
                            )
                for when, hook in hooks:

                    @pl.when(h * 16 + i == when)
                    def _(hook=hook):
                        hook()

                return tuple(sums)

            sums = lax.fori_loop(0, WX // 2, rows_step, tuple(jnp.zeros((8, 128), F32) for _ in range(7 * n)))
            for t in range(7 * n):
                kg_ref[h, pl.ds((a0 * 7 + t) * 8, 8), :] = sums[t]
            return c

        lax.fori_loop(0, 2, half_step, 0)

    taps(0, 4, ((16, first[2]),))
    taps(4, 3, ((10, second[2]),))

    for h in range(2):
        total = kg_ref[h, pl.ds(0, 64, stride=8), :]
        for s in range(1, 8):
            total = total + kg_ref[h, pl.ds(s, 64, stride=8), :]
        v_ref[h * 64 : h * 64 + 64, :] = total

    def small_rc(src, dst, k, dev):
        return pltpu.make_async_remote_copy(
            src_ref=src, dst_ref=dst, send_sem=vs_sem.at[k], recv_sem=vr_sem.at[k], device_id=dev,
            device_id_type=MESH,
        )

    def small_in(k):
        return small_rc(v_ref.at[block8(at_sx(k))], vr_ref.at[block8(sx)], k, {"sx": at_sx(k)})

    def small_z(k):
        return small_rc(vz_ref.at[sy], vz_ref.at[sy], 15 + k, {"sy": at_sy(k)})

    def small_out(k):
        return small_rc(vf_ref.at[block8(sx)], vf_ref.at[block8(sx)], 18 + k, {"sx": at_sx(k)})

    def each(make, act):
        def body(k, c):
            act(make(k))
            return c

        return body

    def small_step0():
        lax.fori_loop(1, N_SX, each(small_in, lambda copy: copy.start()), 0)
        vr_ref[block8(sx), :] = v_ref[block8(sx), :]

    def small_step1():
        lax.fori_loop(1, N_SX, each(small_in, lambda copy: copy.wait()), 0)
        vz_ref[sy] = jnp.sum(vr_ref[...].reshape(16, 8, 128), axis=0)
        for k in range(1, N_SY):
            small_z(k).start()

    def small_step2():
        for k in range(1, N_SY):
            small_z(k).wait()
        vf_ref[block8(sx), :] = (vz_ref[0] + vz_ref[1]) + (vz_ref[2] + vz_ref[3])
        lax.fori_loop(1, N_SX, each(small_out, lambda copy: copy.start()), 0)

    def small_step3():
        lax.fori_loop(1, N_SX, each(small_out, lambda copy: copy.wait()), 0)
        small_ref[...] = vf_ref[...]

    small_step0()

    for copy in halo_copies(1):
        copy.wait()
    unpack_sides(1, pg_ref)
    unpack_ends(1, pg_ref)

    def back_step(i, c):
        x = i * 2
        keep = mv_ref[x // 8]
        for h in range(2):
            sums = depthwise(pg_ref, h, x, True)
            for k in range(2):
                for q in range(4):
                    value = (sums[k][q] + gs_ref[h, block8((x + k) * 4 + q), :]) * keep
                    nat_ref[h, x + k, pl.ds(q, 8, stride=4), :] = value
        for k in range(2):
            gf_ref[x + k] = jnp.concatenate([nat_ref[0, x + k], nat_ref[1, x + k]], axis=1).astype(BF16)

        for when, hook in ((4, first[3]), (12, second[3])):

            @pl.when(i == when)
            def _(hook=hook):
                hook()

        return c

    lax.fori_loop(0, WX // 2, back_step, 0)
    gf_out = pltpu.make_async_copy(gf_ref, gf_hbm, res_sem.at[1])
    gf_out.start()
    small_step1()
    first[4]()
    second[4]()
    small_step2()
    first[5]()
    second[5]()
    small_step3()
    small_out_copy = pltpu.make_async_copy(small_ref, small_hbm, res_sem.at[2])
    small_out_copy.start()
    first[6]()
    second[6]()
    pooled_out.wait()
    gf_out.wait()
    small_out_copy.wait()
    first[7]()
    second[7]()


def finish_kernel(
    pooled_hbm, gf_hbm, small_hbm, expand_hbm, project_hbm, down_hbm,
    pooled_ref, gf_ref, cw_ref, expand_ref, project_ref, down_ref, vec_ref, eb_ref, do_ref,
    gf_in, pooled_in, small_in, expand_in, project_in, down_in, big_ref, in_sem, sem,
):
    pairs = ((down_hbm, down_in, down_ref), (project_hbm, project_in, project_ref), (expand_hbm, expand_in, expand_ref))
    loads = [pltpu.make_async_copy(src, dst, in_sem.at[k]) for k, (src, dst, _) in enumerate(pairs)]
    loads.append(pltpu.make_async_copy(pooled_hbm, pooled_in, in_sem.at[3]))
    loads.append(pltpu.make_async_copy(small_hbm, small_in, in_sem.at[4]))
    loads.append(pltpu.make_async_copy(gf_hbm, gf_in, in_sem.at[5]))
    for load in loads:
        load.start()
    copies = []
    at = 0
    for load, (_, src, dst) in zip(loads, pairs):
        load.wait()
        rows, lanes = src.shape
        step = 65536 // lanes * 2
        for i in range(0, rows, step):
            k = len(copies)
            view = big_ref.at[pl.ds(at, step), pl.ds(0, lanes)]
            view[...] = src[i : i + step, :].astype(F32)
            copies.append(pltpu.make_async_copy(view, dst.at[pl.ds(i, step)], sem.at[k]))
            copies[-1].start()
            at += step
    loads[5].wait()
    copies.append(pltpu.make_async_copy(gf_in, gf_ref, sem.at[len(copies)]))
    copies[-1].start()
    loads[3].wait()
    loads[4].wait()
    for tx in range(4):
        for ty in range(4):
            pooled_ref[tx, ty : ty + 1, :] = pooled_in[tx * 8 + ty * 2 : tx * 8 + ty * 2 + 1, :].astype(BF16)
    for h in range(2):
        cols = slice(h * 128, h * 128 + 128)
        for a in range(7):
            cw_ref[a, :, cols] = small_in[h * 64 + a * 7 : h * 64 + a * 7 + 7, :]
        vec_ref[:, cols] = small_in[h * 64 + 49 : h * 64 + 56, :]
        for q in range(4):
            eb_ref[:, q * 256 + h * 128 : q * 256 + h * 128 + 128] = small_in[h * 64 + 56 + q : h * 64 + 57 + q, :]
        for q in range(2):
            do_ref[:, q * 256 + h * 128 : q * 256 + h * 128 + 128] = small_in[h * 64 + 60 + q : h * 64 + 61 + q, :]
    for copy in copies:
        copy.wait()


def finish(pooled, grad_features, small, expand, project, down):
    vmem = pl.BlockSpec(memory_space=pltpu.VMEM)
    hbm = pl.BlockSpec(memory_space=pl.ANY)
    out = pl.pallas_call(
        finish_kernel,
        out_shape=(
            jax.ShapeDtypeStruct((4, 4, 512), BF16),
            jax.ShapeDtypeStruct((WX, WY, 256), BF16),
            jax.ShapeDtypeStruct((7, 7, 256), F32),
            jax.ShapeDtypeStruct((256, 1024), F32),
            jax.ShapeDtypeStruct((1024, 256), F32),
            jax.ShapeDtypeStruct((1024, 512), F32),
            jax.ShapeDtypeStruct((7, 256), F32),
            jax.ShapeDtypeStruct((1, 1024), F32),
            jax.ShapeDtypeStruct((1, 512), F32),
        ),
        in_specs=[hbm] * 6,
        out_specs=(vmem, hbm, vmem, hbm, hbm, hbm, vmem, vmem, vmem),
        scratch_shapes=[
            pltpu.VMEM((WX, WY, 256), BF16), pltpu.VMEM((32, 512), F32), pltpu.VMEM((128, 128), F32),
            pltpu.VMEM((256, 1024), BF16),
            pltpu.VMEM((1024, 256), BF16), pltpu.VMEM((1024, 512), BF16), pltpu.VMEM((2304, 1024), F32),
            pltpu.SemaphoreType.DMA((6,)), pltpu.SemaphoreType.DMA((16,)),
        ],
        compiler_params=pltpu.CompilerParams(vmem_limit_bytes=60 * 1024 * 1024),
        cost_estimate=pl.CostEstimate(flops=1_000_000, bytes_accessed=7_000_000, transcendentals=0),
    )(pooled, grad_features, small, expand, project, down)
    return out[:7] + (out[7].reshape(1024), out[8].reshape(512))


def on_device(
    features,
    return_slot,
    returned_grads,
    conv_weight,
    conv_bias,
    norm_gain,
    norm_bias,
    expand_weight,
    expand_bias,
    project_weight,
    project_bias,
    layer_scale,
    down_gain,
    down_bias,
    down_weight,
    down_offset,
):
    hbm = pl.BlockSpec(memory_space=pl.ANY)

    def row(v):
        return v.reshape(1, -1)

    def vm(*shape, dtype=F32):
        return pltpu.VMEM(shape, dtype)

    dma = pltpu.SemaphoreType.DMA
    parts = pl.pallas_call(
        kernel,
        out_shape=(
            jax.ShapeDtypeStruct((32, 512), F32),
            jax.ShapeDtypeStruct((WX, WY, 256), BF16),
            jax.ShapeDtypeStruct((128, 128), F32),
            jax.ShapeDtypeStruct((256, 1024), BF16),
            jax.ShapeDtypeStruct((1024, 256), BF16),
            jax.ShapeDtypeStruct((1024, 512), BF16),
        ),
        in_specs=[hbm] * 16,
        out_specs=(hbm,) * 6,
        scratch_shapes=[
            pltpu.SMEM((4, 4), jnp.int32), vm(WX, WY, 256, dtype=BF16), vm(32, 512, dtype=BF16), vm(7, 7, 256),
            vm(1, 256), vm(1, 256), vm(1, 256), vm(256, 1024, dtype=BF16), vm(1, 1024), vm(1024, 256, dtype=BF16),
            vm(1, 256), vm(1, 256), vm(1, 256), vm(1, 256), vm(1024, 512, dtype=BF16), vm(1, 512),
            vm(32, 512), vm(WX, WY, 256, dtype=BF16), vm(128, 128), dma((16,)), dma((3,)),
            vm(2, PLANE, 128), vm(2, PLANE, 128), vm(2, 2, 2, 3, 32, 128, dtype=BF16),
            vm(2, 2, 2, 3, 32, 128, dtype=BF16), vm(2, 2, 2, 3, 32, 128, dtype=BF16),
            vm(2, 2, 2, 3, 32, 128, dtype=BF16), vm(2, 4, 2, 3, 16, 128, dtype=BF16),
            vm(2, 49, 8, 128), vm(4, 32, 128), vm(4, 8, 128),
            vm(4, 32, 128), vm(128, 128), vm(128, 128), vm(4, 32, 128), vm(32, 512, dtype=BF16), vm(4, 8, 1024),
            vm(4, 32, 256),
            vm(2, 1024, 128), vm(1024, 256), vm(1024, 128), vm(256, 1024, dtype=BF16), vm(256, 1024, dtype=BF16),
            vm(1024, 1024, dtype=BF16), vm(1024, 1024, dtype=BF16),
            vm(1024, 1024), vm(2, 1024, 128), vm(1024, 256, dtype=BF16), vm(2, 32, 32, 128),
            vm(2, 512, 128), vm(128, 128), vm(128, 128), vm(4, 8, 128), vm(128, 128),
            vm(2, 2048, 256), vm(2, 1024, 256, dtype=BF16), vm(2, 1024, 256, dtype=BF16),
            vm(2, 1024, 256, dtype=BF16), vm(2, 2, 3, 128, 256, dtype=BF16),
            vm(2, 2, 128, 256, dtype=BF16), vm(2, 2, 7, 16, 256, dtype=BF16), vm(2, 2048, 256, dtype=BF16),
            dma((2, 8)), dma((2, 8)), dma((16,)), dma((16,)), dma((2, 52)), dma((2, 52)), dma((34,)), dma((34,)),
            dma((2, 5)),
        ],
        compiler_params=pltpu.CompilerParams(
            collective_id=0, has_side_effects=True, vmem_limit_bytes=60 * 1024 * 1024
        ),
        cost_estimate=pl.CostEstimate(flops=4_000_000_000, bytes_accessed=8_000_000, transcendentals=1_000_000),
    )(
        return_slot, features, returned_grads[0], conv_weight, row(conv_bias), row(norm_gain), row(norm_bias),
        expand_weight, row(expand_bias), project_weight, row(project_bias), row(layer_scale), row(down_gain),
        row(down_bias), down_weight, row(down_offset),
    )
    return finish(*parts)


def solution(mesh):
    placed = (
        P(("slide", "sx"), "sy", None),
        P(("slide", "sx"), "sy"),
        P("sy", ("slide", "sx"), None),
    ) + (P(),) * 13
    return jax.shard_map(
        on_device,
        mesh=mesh,
        in_specs=placed,
        out_specs=(
            P(("slide", "sx"), "sy", None),
            P(("slide", "sx"), "sy", None),
            P("slide", None, None),
            P("slide", None),
            P("slide", None),
            P("slide", None),
            P("slide", None),
            P("slide"),
            P("slide"),
        ),
        check_vma=False,
    )
```

time: 91.2 us -> 58.9 us (0.65)
  Pallas kernels: 78.4 us -> 58.1 us
  other arithmetic: 6.64 us -> 0 us
  local copies, waits for them, and re-layouts: 5.15 us -> 0 us
    pallas_call x1, Pallas kernels: 78.4 us -> 53.8 us  [on_device(): pl.pallas_call(kernel, out_shape=(jax.ShapeDtypeStruct((32, 512), F32), j...]
    pallas_call x0 -> x1, Pallas kernels: none -> 4.26 us  [finish(): pl.pallas_call(finish_kernel, out_shape=(jax.ShapeDtypeStruct((4, 4, 512)...]
    convert_element_type x2 -> x0, other arithmetic: 2.7 us -> none  [the longest x1 1.61 us: on_device(): down = jnp.concatenate([big[0, :1024], big[0, 1024:]], axis=1).astype(F32)]
    unnamed x6 -> x0, local copies, waits for them, and re-layouts: 2.59 us -> none
    squeeze x1 -> x0, other arithmetic: 2.48 us -> none  [on_device(): down = jnp.concatenate([big[0, :1024], big[0, 1024:]], axis=1).astype(F32)]
    squeeze x1 -> x0, local copies, waits for them, and re-layouts: 1.13 us -> none  [on_device(): big[1, j * 256:j * 256 + 256]]
where the time goes in v2:
time: 58.9 us; the launch traced here: 58.7 us
  Pallas kernels  58.1 us (99%)
  between operations  0.66 us (1%)
    pallas_call x1, Pallas kernels, on_device(): pl.pallas_call(kernel, out_shape=(jax.ShapeDtypeStruct((32, 512), F32), j...  53.8 us
    pallas_call x1, Pallas kernels, finish(): pl.pallas_call(finish_kernel, out_shape=(jax.ShapeDtypeStruct((4, 4, 512)...  4.26 us

profile of v2, /device:TPU:1, one launch (start us, length us, event | category | flops | bytes accessed | tf_op | source)
XLA Modules:
  0.0 58.7 jit_solution(12391095809622185100)
XLA Ops:
  0.6 53.8 %shard_map.223 = (f32[32,512]{1,0:T(8,128)}, bf16[32,32,256]{2,1,0:T(8,128)(2,1)}, f32[128,128]{1,0:T(8,128)}, bf16[256,1024]{1,0:T(8,128)(2,1)}, bf16[1024,256]{1,0:T(8,128)(2,1)}, /*index=5*/bf16[1024,512]{1,0:T(8,128)(2,1)}) custom-call(s32[4,4]{1,0:T(4,128)} %slot_hbm.1, bf16[32,32,256]{2,1,0:T(8,128)(2,1)} %feat_hbm.1, bf16[32,512]{1,0:T(8,128)(2,1)} %bitcast.12, ...), custom_call_target="tpu_custom_call" | custom-call | flops 4000000000 | bytes 8000000 | tf_op jit(solution)/shard_map/pallas_call | solution.py:845
  54.5 4.3 %shard_map.224 = (bf16[4,4,512]{2,1,0:T(4,128)(2,1)}, bf16[32,32,256]{2,1,0:T(8,128)(2,1)}, f32[7,7,256]{2,1,0:T(8,128)}, f32[256,1024]{1,0:T(8,128)}, f32[1024,...) custom-call(f32[32,512]{1,0:T(8,128)} %get-tuple-element.24.pooled_hbm, ...), custom_call_target="tpu_custom_call" | custom-call | flops 1000000 | bytes 7000000 | tf_op jit(solution)/shard_map/pallas_call | solution.py:791

commit v3 on v2

--- a/solution.py
+++ b/solution.py
@@ -339,7 +339,7 @@
         return jnp.concatenate(row * 4, axis=0)
 
     def forward(tx, c):
-        rows = pl.ds(pl.multiple_of(tx * 256, 256), 256)
+        rows = pl.ds(tx * 256, 256)
         v = jnp.concatenate([co_ref[0, rows, :], co_ref[1, rows, :]], axis=1)
         shifted = v - row_mean(v)
         inv = lax.rsqrt(row_mean(shifted * shifted) + norm_eps)
@@ -398,7 +398,8 @@
         nit_ref[:, rows] = normed_in.T
         return c
 
-    lax.fori_loop(0, 4, forward, 0)
+    for tx in range(4):
+        forward(tx, 0)
 
     def batch(b):
         core_dev = {"sx": sx + 1 - 2 * core}
@@ -571,14 +572,17 @@
         loc_ref[1, 1024 + j * 256 : 1024 + j * 256 + 256, :] = mm(gbt_ref[...], act_ref[:, cols], 1, 0).T
 
     hidden_back(0)
+    second[0]((0,))
     hidden_back(1)
+    second[0]((1,))
     first[1]()
     hidden_back(2)
+    second[0]((2,))
     hidden_back(3)
-    second[0]()
+    second[0]((3,))
 
     def backward(tx, c):
-        rows = pl.ds(pl.multiple_of(tx * 256, 256), 256)
+        rows = pl.ds(tx * 256, 256)
         grad_normed = mm(gh_ref[rows, :], w1_ref[...], 1, 1)
         normed = nc_ref[rows, :]
         add_entry(50, fold8(grad_normed * normed))
@@ -596,13 +600,12 @@
                     at = (x * 4 + q) * 8
                     pg_ref[h, pl.ds((tx * 8 + x + 3) * PITCH + LEFT + q, 8, stride=4), :] = half[at : at + 8, :]
 
-        @pl.when(tx == 1)
-        def _():
-            second[1]()
-
-        return c
-
-    lax.fori_loop(0, 4, backward, 0)
+        return c
+
+    backward(0, 0)
+    second[1]()
+    for tx in range(1, 4):
+        backward(tx, 0)
 
     pack(1, pg_ref)
     for copy in halo_copies(1):
@@ -625,23 +628,23 @@
                             sums[a * 7 + b] = sums[a * 7 + b] + (
                                 (rows[b] * g[0] + rows[b + 1] * g[1]) + (rows[b + 2] * g[2] + rows[b + 3] * g[3])
                             )
-                for when, hook in hooks:
-
-                    @pl.when(h * 16 + i == when)
-                    def _(hook=hook):
-                        hook()
-
                 return tuple(sums)
 
             sums = lax.fori_loop(0, WX // 2, rows_step, tuple(jnp.zeros((8, 128), F32) for _ in range(7 * n)))
             for t in range(7 * n):
                 kg_ref[h, pl.ds((a0 * 7 + t) * 8, 8), :] = sums[t]
+            for when, hook in hooks:
+
+                @pl.when(h == when)
+                def _(hook=hook):
+                    hook()
+
             return c
 
         lax.fori_loop(0, 2, half_step, 0)
 
-    taps(0, 4, ((16, first[2]),))
-    taps(4, 3, ((10, second[2]),))
+    taps(0, 4, ((0, first[2]),))
+    taps(4, 3, ((0, second[2]),))
 
     for h in range(2):
         total = kg_ref[h, pl.ds(0, 64, stride=8), :]
@@ -710,15 +713,19 @@
         for k in range(2):
             gf_ref[x + k] = jnp.concatenate([nat_ref[0, x + k], nat_ref[1, x + k]], axis=1).astype(BF16)
 
-        for when, hook in ((4, first[3]), (12, second[3])):
-
-            @pl.when(i == when)
+        return c
+
+    def back_part(g, c):
+        lax.fori_loop(g * 4, g * 4 + 4, back_step, 0)
+        for when, hook in ((0, first[3]), (2, second[3]),):
+
+            @pl.when(g == when)
             def _(hook=hook):
                 hook()
 
         return c
 
-    lax.fori_loop(0, WX // 2, back_step, 0)
+    lax.fori_loop(0, 4, back_part, 0)
     gf_out = pltpu.make_async_copy(gf_ref, gf_hbm, res_sem.at[1])
     gf_out.start()
     small_step1()
@@ -741,37 +748,41 @@
 
 def finish_kernel(
     pooled_hbm, gf_hbm, small_hbm, expand_hbm, project_hbm, down_hbm,
-    pooled_ref, gf_ref, cw_ref, expand_ref, project_ref, down_ref, vec_ref, eb_ref, do_ref,
-    gf_in, pooled_in, small_in, expand_in, project_in, down_in, big_ref, in_sem, sem,
+    pooled_out, gf_out, cw_out, expand_out, project_out, down_out, vec_out, eb_out, do_out,
+    gf_in, pooled_in, small_in, expand_in, project_in, down_in, big_ref,
+    pooled_ref, cw_ref, vec_ref, eb_ref, do_ref, in_sem, sem,
 ):
-    pairs = ((down_hbm, down_in, down_ref), (project_hbm, project_in, project_ref), (expand_hbm, expand_in, expand_ref))
-    loads = [pltpu.make_async_copy(src, dst, in_sem.at[k]) for k, (src, dst, _) in enumerate(pairs)]
-    loads.append(pltpu.make_async_copy(pooled_hbm, pooled_in, in_sem.at[3]))
-    loads.append(pltpu.make_async_copy(small_hbm, small_in, in_sem.at[4]))
-    loads.append(pltpu.make_async_copy(gf_hbm, gf_in, in_sem.at[5]))
-    for load in loads:
-        load.start()
-    copies = []
-    at = 0
-    for load, (_, src, dst) in zip(loads, pairs):
-        load.wait()
+    loads = []
+
+    def load(src, dst):
+        loads.append(pltpu.make_async_copy(src, dst, in_sem.at[len(loads)]))
+        loads[-1].start()
+
+    stores = []
+
+    def store(src, dst):
+        stores.append(pltpu.make_async_copy(src, dst, sem.at[len(stores)]))
+        stores[-1].start()
+
+    load(pooled_hbm, pooled_in)
+    load(small_hbm, small_in)
+    pieces = []
+    for src, mid, dst in (
+        (down_hbm, down_in, down_out), (project_hbm, project_in, project_out), (expand_hbm, expand_in, expand_out)
+    ):
         rows, lanes = src.shape
-        step = 65536 // lanes * 2
+        step = 131072 // lanes
         for i in range(0, rows, step):
-            k = len(copies)
-            view = big_ref.at[pl.ds(at, step), pl.ds(0, lanes)]
-            view[...] = src[i : i + step, :].astype(F32)
-            copies.append(pltpu.make_async_copy(view, dst.at[pl.ds(i, step)], sem.at[k]))
-            copies[-1].start()
-            at += step
-    loads[5].wait()
-    copies.append(pltpu.make_async_copy(gf_in, gf_ref, sem.at[len(copies)]))
-    copies[-1].start()
-    loads[3].wait()
-    loads[4].wait()
+            load(src.at[pl.ds(i, step)], mid.at[pl.ds(i, step)])
+            pieces.append((mid, dst, i, step, lanes))
+    load(gf_hbm, gf_in)
+
+    loads[0].wait()
     for tx in range(4):
         for ty in range(4):
             pooled_ref[tx, ty : ty + 1, :] = pooled_in[tx * 8 + ty * 2 : tx * 8 + ty * 2 + 1, :].astype(BF16)
+    store(pooled_ref, pooled_out)
+    loads[1].wait()
     for h in range(2):
         cols = slice(h * 128, h * 128 + 128)
         for a in range(7):
@@ -781,12 +792,22 @@
             eb_ref[:, q * 256 + h * 128 : q * 256 + h * 128 + 128] = small_in[h * 64 + 56 + q : h * 64 + 57 + q, :]
         for q in range(2):
             do_ref[:, q * 256 + h * 128 : q * 256 + h * 128 + 128] = small_in[h * 64 + 60 + q : h * 64 + 61 + q, :]
-    for copy in copies:
+    for src, dst in ((cw_ref, cw_out), (vec_ref, vec_out), (eb_ref, eb_out), (do_ref, do_out)):
+        store(src, dst)
+    at = 0
+    for k, (mid, dst, i, step, lanes) in enumerate(pieces):
+        loads[2 + k].wait()
+        view = big_ref.at[pl.ds(at, step), pl.ds(0, lanes)]
+        view[...] = mid[i : i + step, :].astype(F32)
+        store(view, dst.at[pl.ds(i, step)])
+        at += step
+    loads[-1].wait()
+    store(gf_in, gf_out)
+    for copy in stores:
         copy.wait()
 
 
 def finish(pooled, grad_features, small, expand, project, down):
-    vmem = pl.BlockSpec(memory_space=pltpu.VMEM)
     hbm = pl.BlockSpec(memory_space=pl.ANY)
     out = pl.pallas_call(
         finish_kernel,
@@ -802,12 +823,14 @@
             jax.ShapeDtypeStruct((1, 512), F32),
         ),
         in_specs=[hbm] * 6,
-        out_specs=(vmem, hbm, vmem, hbm, hbm, hbm, vmem, vmem, vmem),
+        out_specs=(hbm,) * 9,
         scratch_shapes=[
             pltpu.VMEM((WX, WY, 256), BF16), pltpu.VMEM((32, 512), F32), pltpu.VMEM((128, 128), F32),
             pltpu.VMEM((256, 1024), BF16),
             pltpu.VMEM((1024, 256), BF16), pltpu.VMEM((1024, 512), BF16), pltpu.VMEM((2304, 1024), F32),
-            pltpu.SemaphoreType.DMA((6,)), pltpu.SemaphoreType.DMA((16,)),
+            pltpu.VMEM((4, 4, 512), BF16), pltpu.VMEM((7, 7, 256), F32), pltpu.VMEM((7, 256), F32),
+            pltpu.VMEM((1, 1024), F32), pltpu.VMEM((1, 512), F32),
+            pltpu.SemaphoreType.DMA((11,)), pltpu.SemaphoreType.DMA((14,)),
         ],
         compiler_params=pltpu.CompilerParams(vmem_limit_bytes=60 * 1024 * 1024),
         cost_estimate=pl.CostEstimate(flops=1_000_000, bytes_accessed=7_000_000, transcendentals=0),

time: 58.9 us -> 56.3 us (0.956)
  Pallas kernels: 58.1 us -> 55.5 us
    pallas_call x1, Pallas kernels: 53.8 us -> 52 us  [on_device(): pl.pallas_call(kernel, out_shape=(jax.ShapeDtypeStruct((32, 512), F32), j...]
    pallas_call x1, Pallas kernels: 4.26 us -> 3.46 us  [finish(): pl.pallas_call(finish_kernel, out_shape=(jax.ShapeDtypeStruct((4, 4, 512)...]
where the time goes in v3:
time: 56.3 us; the launch traced here: 56.2 us
  Pallas kernels  55.5 us (99%)
  between operations  0.66 us (1%)
    pallas_call x1, Pallas kernels, on_device(): pl.pallas_call(kernel, out_shape=(jax.ShapeDtypeStruct((32, 512), F32), j...  52 us
    pallas_call x1, Pallas kernels, finish(): pl.pallas_call(finish_kernel, out_shape=(jax.ShapeDtypeStruct((4, 4, 512)...  3.46 us

profile of v3, /device:TPU:1, one launch (start us, length us, event | category | flops | bytes accessed | tf_op | source)
XLA Modules:
  0.0 56.2 jit_solution(5329071932107660066)
XLA Ops:
  0.6 52.0 %shard_map.223 = (f32[32,512]{1,0:T(8,128)}, bf16[32,32,256]{2,1,0:T(8,128)(2,1)}, f32[128,128]{1,0:T(8,128)}, bf16[256,1024]{1,0:T(8,128)(2,1)}, bf16[1024,256]{1,0:T(8,128)(2,1)}, /*index=5*/bf16[1024,512]{1,0:T(8,128)(2,1)}) custom-call(s32[4,4]{1,0:T(4,128)} %slot_hbm.1, bf16[32,32,256]{2,1,0:T(8,128)(2,1)} %feat_hbm.1, bf16[32,512]{1,0:T(8,128)(2,1)} %bitcast.12, ...), custom_call_target="tpu_custom_call" | custom-call | flops 4000000000 | bytes 8000000 | tf_op jit(solution)/shard_map/pallas_call | solution.py:868
  52.7 3.5 %shard_map.224 = (bf16[4,4,512]{2,1,0:T(4,128)(2,1)}, bf16[32,32,256]{2,1,0:T(8,128)(2,1)}, f32[7,7,256]{2,1,0:T(8,128)}, f32[256,1024]{1,0:T(8,128)}, f32[1024,...) custom-call(f32[32,512]{1,0:T(8,128)} %get-tuple-element.24.pooled_hbm, ...), custom_call_target="tpu_custom_call" | custom-call | flops 1000000 | bytes 7000000 | tf_op jit(solution)/shard_map/pallas_call | solution.py:812

commit v4 on v3

--- a/solution.py
+++ b/solution.py
@@ -39,9 +39,9 @@
 def kernel(
     slot_hbm, feat_hbm, ret_hbm, cw_hbm, cb_hbm, ng_hbm, nb_hbm, w1_hbm, b1_hbm, w2_hbm, b2_hbm, ls_hbm, dg_hbm,
     db_hbm, dw_hbm, do_hbm,
-    pooled_hbm, gf_hbm, small_hbm, expand_ref, project_ref, down_ref,
+    pooled_ref, gf_ref, small_ref, expand_ref, project_ref, down_ref,
     slot_ref, feat_ref, ret_ref, cw_ref, cb_ref, ng_ref, nb_ref, w1_ref, b1_ref, w2_ref, b2_ref, ls_ref, dg_ref,
-    db_ref, dw_ref, do_ref, pooled_ref, gf_ref, small_ref, in_sem, res_sem,
+    db_ref, dw_ref, do_ref, in_sem,
     p_ref, pg_ref, xp_ref, xr_ref, yp_ref, yr_ref, cr_ref, wb_ref, mn_ref, mv_ref,
     rg_ref, pk_ref, rv_ref, ar_ref, gr_ref, gp_ref, ps_ref,
     co_ref, nc_ref, inv_ref, nit_ref, gbt_ref, gh_ref, act_ref, sl_ref, gs_ref, gb_ref, nat_ref,
@@ -558,8 +558,6 @@
         pool = part if pool is None else pool + part
     tissue = jnp.concatenate([mv_ref[...].reshape(32, 128)] * 4, axis=1)
     pooled_ref[...] = (pool * (1.0 / 16.0) + do_ref[...]) * tissue
-    pooled_out = pltpu.make_async_copy(pooled_ref, pooled_hbm, res_sem.at[0])
-    pooled_out.start()
     first[0]()
 
     def hidden_back(j):
@@ -726,8 +724,6 @@
         return c
 
     lax.fori_loop(0, 4, back_part, 0)
-    gf_out = pltpu.make_async_copy(gf_ref, gf_hbm, res_sem.at[1])
-    gf_out.start()
     small_step1()
     first[4]()
     second[4]()
@@ -735,54 +731,41 @@
     first[5]()
     second[5]()
     small_step3()
-    small_out_copy = pltpu.make_async_copy(small_ref, small_hbm, res_sem.at[2])
-    small_out_copy.start()
     first[6]()
     second[6]()
-    pooled_out.wait()
-    gf_out.wait()
-    small_out_copy.wait()
     first[7]()
     second[7]()
 
 
 def finish_kernel(
-    pooled_hbm, gf_hbm, small_hbm, expand_hbm, project_hbm, down_hbm,
+    pooled_in, gf_in, small_in, expand_in, project_in, down_in,
     pooled_out, gf_out, cw_out, expand_out, project_out, down_out, vec_out, eb_out, do_out,
-    gf_in, pooled_in, small_in, expand_in, project_in, down_in, big_ref,
-    pooled_ref, cw_ref, vec_ref, eb_ref, do_ref, in_sem, sem,
+    big_ref, pooled_ref, cw_ref, vec_ref, eb_ref, do_ref, sem,
 ):
-    loads = []
-
-    def load(src, dst):
-        loads.append(pltpu.make_async_copy(src, dst, in_sem.at[len(loads)]))
-        loads[-1].start()
-
     stores = []
 
     def store(src, dst):
         stores.append(pltpu.make_async_copy(src, dst, sem.at[len(stores)]))
         stores[-1].start()
 
-    load(pooled_hbm, pooled_in)
-    load(small_hbm, small_in)
+    store(gf_in, gf_out)
     pieces = []
-    for src, mid, dst in (
-        (down_hbm, down_in, down_out), (project_hbm, project_in, project_out), (expand_hbm, expand_in, expand_out)
-    ):
+    for src, dst in ((down_in, down_out), (project_in, project_out), (expand_in, expand_out)):
         rows, lanes = src.shape
         step = 131072 // lanes
         for i in range(0, rows, step):
-            load(src.at[pl.ds(i, step)], mid.at[pl.ds(i, step)])
-            pieces.append((mid, dst, i, step, lanes))
-    load(gf_hbm, gf_in)
-
-    loads[0].wait()
+            pieces.append((src, dst, i, step, lanes))
+
+    at = 0
+    for mid, dst, i, step, lanes in pieces:
+        view = big_ref.at[pl.ds(at, step), pl.ds(0, lanes)]
+        view[...] = mid[i : i + step, :].astype(F32)
+        store(view, dst.at[pl.ds(i, step)])
+        at += step
     for tx in range(4):
         for ty in range(4):
             pooled_ref[tx, ty : ty + 1, :] = pooled_in[tx * 8 + ty * 2 : tx * 8 + ty * 2 + 1, :].astype(BF16)
     store(pooled_ref, pooled_out)
-    loads[1].wait()
     for h in range(2):
         cols = slice(h * 128, h * 128 + 128)
         for a in range(7):
@@ -794,15 +777,6 @@
             do_ref[:, q * 256 + h * 128 : q * 256 + h * 128 + 128] = small_in[h * 64 + 60 + q : h * 64 + 61 + q, :]
     for src, dst in ((cw_ref, cw_out), (vec_ref, vec_out), (eb_ref, eb_out), (do_ref, do_out)):
         store(src, dst)
-    at = 0
-    for k, (mid, dst, i, step, lanes) in enumerate(pieces):
-        loads[2 + k].wait()
-        view = big_ref.at[pl.ds(at, step), pl.ds(0, lanes)]
-        view[...] = mid[i : i + step, :].astype(F32)
-        store(view, dst.at[pl.ds(i, step)])
-        at += step
-    loads[-1].wait()
-    store(gf_in, gf_out)
     for copy in stores:
         copy.wait()
 
@@ -822,17 +796,15 @@
             jax.ShapeDtypeStruct((1, 1024), F32),
             jax.ShapeDtypeStruct((1, 512), F32),
         ),
-        in_specs=[hbm] * 6,
+        in_specs=[pl.BlockSpec(memory_space=pltpu.VMEM)] * 6,
         out_specs=(hbm,) * 9,
         scratch_shapes=[
-            pltpu.VMEM((WX, WY, 256), BF16), pltpu.VMEM((32, 512), F32), pltpu.VMEM((128, 128), F32),
-            pltpu.VMEM((256, 1024), BF16),
-            pltpu.VMEM((1024, 256), BF16), pltpu.VMEM((1024, 512), BF16), pltpu.VMEM((2304, 1024), F32),
+            pltpu.VMEM((2304, 1024), F32),
             pltpu.VMEM((4, 4, 512), BF16), pltpu.VMEM((7, 7, 256), F32), pltpu.VMEM((7, 256), F32),
             pltpu.VMEM((1, 1024), F32), pltpu.VMEM((1, 512), F32),
-            pltpu.SemaphoreType.DMA((11,)), pltpu.SemaphoreType.DMA((14,)),
+            pltpu.SemaphoreType.DMA((14,)),
         ],
-        compiler_params=pltpu.CompilerParams(vmem_limit_bytes=60 * 1024 * 1024),
+        compiler_params=pltpu.CompilerParams(vmem_limit_bytes=24 * 1024 * 1024),
         cost_estimate=pl.CostEstimate(flops=1_000_000, bytes_accessed=7_000_000, transcendentals=0),
     )(pooled, grad_features, small, expand, project, down)
     return out[:7] + (out[7].reshape(1024), out[8].reshape(512))
@@ -868,20 +840,20 @@
     parts = pl.pallas_call(
         kernel,
         out_shape=(
-            jax.ShapeDtypeStruct((32, 512), F32),
-            jax.ShapeDtypeStruct((WX, WY, 256), BF16),
-            jax.ShapeDtypeStruct((128, 128), F32),
-            jax.ShapeDtypeStruct((256, 1024), BF16),
-            jax.ShapeDtypeStruct((1024, 256), BF16),
-            jax.ShapeDtypeStruct((1024, 512), BF16),
+            pltpu.VMEM((32, 512), F32),
+            pltpu.VMEM((WX, WY, 256), BF16),
+            pltpu.VMEM((128, 128), F32),
+            pltpu.VMEM((256, 1024), BF16),
+            pltpu.VMEM((1024, 256), BF16),
+            pltpu.VMEM((1024, 512), BF16),
         ),
-        in_specs=[hbm] * 16,
-        out_specs=(hbm,) * 6,
+        in_specs=[pl.BlockSpec(memory_space=pltpu.HBM)] * 16,
+        out_specs=(pl.BlockSpec(memory_space=pltpu.VMEM),) * 6,
         scratch_shapes=[
             pltpu.SMEM((4, 4), jnp.int32), vm(WX, WY, 256, dtype=BF16), vm(32, 512, dtype=BF16), vm(7, 7, 256),
             vm(1, 256), vm(1, 256), vm(1, 256), vm(256, 1024, dtype=BF16), vm(1, 1024), vm(1024, 256, dtype=BF16),
             vm(1, 256), vm(1, 256), vm(1, 256), vm(1, 256), vm(1024, 512, dtype=BF16), vm(1, 512),
-            vm(32, 512), vm(WX, WY, 256, dtype=BF16), vm(128, 128), dma((16,)), dma((3,)),
+            dma((16,)),
             vm(2, PLANE, 128), vm(2, PLANE, 128), vm(2, 2, 2, 3, 32, 128, dtype=BF16),
             vm(2, 2, 2, 3, 32, 128, dtype=BF16), vm(2, 2, 2, 3, 32, 128, dtype=BF16),
             vm(2, 2, 2, 3, 32, 128, dtype=BF16), vm(2, 4, 2, 3, 16, 128, dtype=BF16),
@@ -899,13 +871,15 @@
             dma((2, 5)),
         ],
         compiler_params=pltpu.CompilerParams(
-            collective_id=0, has_side_effects=True, vmem_limit_bytes=60 * 1024 * 1024
+            collective_id=0, has_side_effects=True, vmem_limit_bytes=48 * 1024 * 1024
         ),
         cost_estimate=pl.CostEstimate(flops=4_000_000_000, bytes_accessed=8_000_000, transcendentals=1_000_000),
     )(
+        *(pltpu.with_memory_space_constraint(v, pltpu.HBM) for v in (
         return_slot, features, returned_grads[0], conv_weight, row(conv_bias), row(norm_gain), row(norm_bias),
         expand_weight, row(expand_bias), project_weight, row(project_bias), row(layer_scale), row(down_gain),
         row(down_bias), down_weight, row(down_offset),
+        ))
     )
     return finish(*parts)
 

time: 56.3 us -> 54.3 us (0.964)
  Pallas kernels: 55.5 us -> 53.5 us
    pallas_call x1, Pallas kernels: 3.46 us -> 2.31 us  [finish(): pl.pallas_call(finish_kernel, out_shape=(jax.ShapeDtypeStruct((4, 4, 512)...]
    pallas_call x1, Pallas kernels: 52 us -> 51.2 us  [on_device(): pl.pallas_call(kernel, out_shape=(pltpu.VMEM((32, 512), F32), pltpu.VMEM(...]
where the time goes in v4:
time: 54.3 us; the launch traced here: 54.1 us
  Pallas kernels  53.5 us (99%)
  between operations  0.66 us (1%)
    pallas_call x1, Pallas kernels, on_device(): pl.pallas_call(kernel, out_shape=(pltpu.VMEM((32, 512), F32), pltpu.VMEM(...  51.2 us
    pallas_call x1, Pallas kernels, finish(): pl.pallas_call(finish_kernel, out_shape=(jax.ShapeDtypeStruct((4, 4, 512)...  2.31 us

profile of v4, /device:TPU:1, one launch (start us, length us, event | category | flops | bytes accessed | tf_op | source)
XLA Modules:
  0.0 54.1 jit_solution(12902134647748425788)
XLA Ops:
  0.6 51.2 %shard_map.223 = (f32[32,512]{1,0:T(8,128)S(1)}, bf16[32,32,256]{2,1,0:T(8,128)(2,1)S(1)}, f32[128,128]{1,0:T(8,128)S(1)}, bf16[256,1024]{1,0:T(8,128)(2,1)S(1)}...) custom-call(s32[4,4]{1,0:T(4,128)} %slot_hbm.1, bf16[32,32,256]{2,1,0:T(8,128)(2,1)} %feat_hbm.1, ...), custom_call_target="tpu_custom_call" | custom-call | flops 4000000000 | bytes 8000000 | tf_op jit(solution)/shard_map/pallas_call | solution.py:840
  51.8 2.3 %shard_map.224 = (bf16[4,4,512]{2,1,0:T(4,128)(2,1)}, bf16[32,32,256]{2,1,0:T(8,128)(2,1)}, f32[7,7,256]{2,1,0:T(8,128)}, f32[256,1024]{1,0:T(8,128)}, f32[1024,...) custom-call(f32[32,512]{1,0:T(8,128)S(1)} %get-tuple-element.24.pooled_in, ...), custom_call_target="tpu_custom_call" | custom-call | flops 1000000 | bytes 7000000 | tf_op jit(solution)/shard_map/pallas_call | solution.py:786

commit v5 on v4

--- a/solution.py
+++ b/solution.py
@@ -39,15 +39,15 @@
 def kernel(
     slot_hbm, feat_hbm, ret_hbm, cw_hbm, cb_hbm, ng_hbm, nb_hbm, w1_hbm, b1_hbm, w2_hbm, b2_hbm, ls_hbm, dg_hbm,
     db_hbm, dw_hbm, do_hbm,
-    pooled_ref, gf_ref, small_ref, expand_ref, project_ref, down_ref,
+    pooled_ref, gf_ref, small_ref, fin_ref,
     slot_ref, feat_ref, ret_ref, cw_ref, cb_ref, ng_ref, nb_ref, w1_ref, b1_ref, w2_ref, b2_ref, ls_ref, dg_ref,
     db_ref, dw_ref, do_ref, in_sem,
     p_ref, pg_ref, xp_ref, xr_ref, yp_ref, yr_ref, cr_ref, wb_ref, mn_ref, mv_ref,
     rg_ref, pk_ref, rv_ref, ar_ref, gr_ref, gp_ref, ps_ref,
     co_ref, nc_ref, inv_ref, nit_ref, gbt_ref, gh_ref, act_ref, sl_ref, gs_ref, gb_ref, nat_ref,
     kg_ref, v_ref, vr_ref, vz_ref, vf_ref,
-    loc_ref, s0_ref, r0_ref, s1_ref, r1_ref, s2_ref, r2_ref, fin_ref,
-    hs_sem, hr_sem, as_sem, ar_sem, bs_sem, br_sem, vs_sem, vr_sem, out_sem,
+    loc_ref, s0_ref, r0_ref, s1_ref, r1_ref, s2_ref, r2_ref,
+    hs_sem, hr_sem, as_sem, ar_sem, bs_sem, br_sem, vs_sem, vr_sem,
 ):
     pairs = (
         (slot_hbm, slot_ref), (feat_hbm, feat_ref), (ret_hbm, ret_ref), (cw_hbm, cw_ref), (cb_hbm, cb_ref),
@@ -511,53 +511,29 @@
                     ring_out(half, k).wait()
                     core_out(half, k).start()
 
-        def out_copies():
-            if b == 0:
-                return [
-                    pltpu.make_async_copy(
-                        fin.at[pl.ds(q * 1024, 1024)], down_ref.at[:, q * 256 : q * 256 + 256], out_sem.at[b, q]
-                    )
-                    for q in range(2)
-                ]
-            return [
-                pltpu.make_async_copy(
-                    fin.at[pl.ds(q * 256, 256)], expand_ref.at[:, q * 256 : q * 256 + 256], out_sem.at[b, q]
-                )
-                for q in range(4)
-            ] + [pltpu.make_async_copy(fin.at[pl.ds(1024, 1024)], project_ref, out_sem.at[b, 4])]
-
         def step6():
             for half in range(2):
                 for k in range(4):
                     core_out(half, k).wait()
-            for copy in out_copies():
-                copy.start()
-
-        def step7():
-            for copy in out_copies():
-                copy.wait()
-
-        return [step0, step1, step2, step3, step4, step5, step6, step7]
+
+        return [step0, step1, step2, step3, step4, step5, step6]
 
     first = batch(0)
     second = batch(1)
 
     gr = gr_ref[...]
     gr2 = jnp.concatenate([gr, gr], axis=0)
-    pool = None
-    for q in range(4):
+
+    def two_terms(q):
         sums = ps_ref[:, q * 8 : q * 8 + 8, :].reshape(32, 256)
         high = sums.astype(BF16)
         low = (sums - high.astype(F32)).astype(BF16)
-        both = jnp.concatenate([high, low], axis=0)
-        grad_down = mm(both, gr2, 0, 0)
+        return jnp.concatenate([high, low], axis=0)
+
+    for q in range(4):
+        grad_down = mm(two_terms(q), gr2, 0, 0)
         loc_ref[0, q * 256 : q * 256 + 256, :] = grad_down[:, :256]
         loc_ref[0, 1024 + q * 256 : 1024 + q * 256 + 256, :] = grad_down[:, 256:]
-        part = mm(both, dw_ref[q * 256 : q * 256 + 256, :], 1, 0)
-        part = part[:32] + part[32:]
-        pool = part if pool is None else pool + part
-    tissue = jnp.concatenate([mv_ref[...].reshape(32, 128)] * 4, axis=1)
-    pooled_ref[...] = (pool * (1.0 / 16.0) + do_ref[...]) * tissue
     first[0]()
 
     def hidden_back(j):
@@ -641,7 +617,8 @@
 
         lax.fori_loop(0, 2, half_step, 0)
 
-    taps(0, 4, ((0, first[2]),))
+    first[2]()
+    taps(0, 4, ())
     taps(4, 3, ((0, second[2]),))
 
     for h in range(2):
@@ -729,16 +706,21 @@
     second[4]()
     small_step2()
     first[5]()
+    pool = None
+    for q in range(4):
+        part = mm(two_terms(q), dw_ref[q * 256 : q * 256 + 256, :], 1, 0)
+        part = part[:32] + part[32:]
+        pool = part if pool is None else pool + part
+    tissue = jnp.concatenate([mv_ref[...].reshape(32, 128)] * 4, axis=1)
+    pooled_ref[...] = (pool * (1.0 / 16.0) + do_ref[...]) * tissue
     second[5]()
     small_step3()
     first[6]()
     second[6]()
-    first[7]()
-    second[7]()
 
 
 def finish_kernel(
-    pooled_in, gf_in, small_in, expand_in, project_in, down_in,
+    pooled_in, gf_in, small_in, sums_in,
     pooled_out, gf_out, cw_out, expand_out, project_out, down_out, vec_out, eb_out, do_out,
     big_ref, pooled_ref, cw_ref, vec_ref, eb_ref, do_ref, sem,
 ):
@@ -749,19 +731,16 @@
         stores[-1].start()
 
     store(gf_in, gf_out)
-    pieces = []
-    for src, dst in ((down_in, down_out), (project_in, project_out), (expand_in, expand_out)):
-        rows, lanes = src.shape
+    at = 0
+    for dst, part, start, blocks in ((down_out, 0, 0, 2), (project_out, 1, 1024, 1), (expand_out, 1, 0, 4)):
+        rows, lanes = dst.shape
         step = 131072 // lanes
         for i in range(0, rows, step):
-            pieces.append((src, dst, i, step, lanes))
-
-    at = 0
-    for mid, dst, i, step, lanes in pieces:
-        view = big_ref.at[pl.ds(at, step), pl.ds(0, lanes)]
-        view[...] = mid[i : i + step, :].astype(F32)
-        store(view, dst.at[pl.ds(i, step)])
-        at += step
+            for q in range(blocks):
+                first = start + q * rows + i
+                big_ref[at : at + step, q * 256 : q * 256 + 256] = sums_in[part, first : first + step, :].astype(F32)
+            store(big_ref.at[pl.ds(at, step), pl.ds(0, lanes)], dst.at[pl.ds(i, step)])
+            at += step
     for tx in range(4):
         for ty in range(4):
             pooled_ref[tx, ty : ty + 1, :] = pooled_in[tx * 8 + ty * 2 : tx * 8 + ty * 2 + 1, :].astype(BF16)
@@ -781,7 +760,7 @@
         copy.wait()
 
 
-def finish(pooled, grad_features, small, expand, project, down):
+def finish(pooled, grad_features, small, sums):
     hbm = pl.BlockSpec(memory_space=pl.ANY)
     out = pl.pallas_call(
         finish_kernel,
@@ -796,7 +775,7 @@
             jax.ShapeDtypeStruct((1, 1024), F32),
             jax.ShapeDtypeStruct((1, 512), F32),
         ),
-        in_specs=[pl.BlockSpec(memory_space=pltpu.VMEM)] * 6,
+        in_specs=[pl.BlockSpec(memory_space=pltpu.VMEM)] * 4,
         out_specs=(hbm,) * 9,
         scratch_shapes=[
             pltpu.VMEM((2304, 1024), F32),
@@ -806,7 +785,7 @@
         ],
         compiler_params=pltpu.CompilerParams(vmem_limit_bytes=24 * 1024 * 1024),
         cost_estimate=pl.CostEstimate(flops=1_000_000, bytes_accessed=7_000_000, transcendentals=0),
-    )(pooled, grad_features, small, expand, project, down)
+    )(pooled, grad_features, small, sums)
     return out[:7] + (out[7].reshape(1024), out[8].reshape(512))
 
 
@@ -843,12 +822,10 @@
             pltpu.VMEM((32, 512), F32),
             pltpu.VMEM((WX, WY, 256), BF16),
             pltpu.VMEM((128, 128), F32),
-            pltpu.VMEM((256, 1024), BF16),
-            pltpu.VMEM((1024, 256), BF16),
-            pltpu.VMEM((1024, 512), BF16),
+            pltpu.VMEM((2, 2048, 256), BF16),
         ),
         in_specs=[pl.BlockSpec(memory_space=pltpu.HBM)] * 16,
-        out_specs=(pl.BlockSpec(memory_space=pltpu.VMEM),) * 6,
+        out_specs=(pl.BlockSpec(memory_space=pltpu.VMEM),) * 4,
         scratch_shapes=[
             pltpu.SMEM((4, 4), jnp.int32), vm(WX, WY, 256, dtype=BF16), vm(32, 512, dtype=BF16), vm(7, 7, 256),
             vm(1, 256), vm(1, 256), vm(1, 256), vm(256, 1024, dtype=BF16), vm(1, 1024), vm(1024, 256, dtype=BF16),
@@ -866,9 +843,8 @@
             vm(2, 512, 128), vm(128, 128), vm(128, 128), vm(4, 8, 128), vm(128, 128),
             vm(2, 2048, 256), vm(2, 1024, 256, dtype=BF16), vm(2, 1024, 256, dtype=BF16),
             vm(2, 1024, 256, dtype=BF16), vm(2, 2, 3, 128, 256, dtype=BF16),
-            vm(2, 2, 128, 256, dtype=BF16), vm(2, 2, 7, 16, 256, dtype=BF16), vm(2, 2048, 256, dtype=BF16),
+            vm(2, 2, 128, 256, dtype=BF16), vm(2, 2, 7, 16, 256, dtype=BF16),
             dma((2, 8)), dma((2, 8)), dma((16,)), dma((16,)), dma((2, 52)), dma((2, 52)), dma((34,)), dma((34,)),
-            dma((2, 5)),
         ],
         compiler_params=pltpu.CompilerParams(
             collective_id=0, has_side_effects=True, vmem_limit_bytes=48 * 1024 * 1024

time: 54.3 us -> 53.8 us (level)
  no operation moved by 1% of the time
where the time goes in v5:
time: 53.8 us; the launch traced here: 53.6 us
  Pallas kernels  53 us (99%)
  between operations  0.66 us (1%)
    pallas_call x1, Pallas kernels, on_device(): pl.pallas_call(kernel, out_shape=(pltpu.VMEM((32, 512), F32), pltpu.VMEM(...  50.7 us
    pallas_call x1, Pallas kernels, finish(): pl.pallas_call(finish_kernel, out_shape=(jax.ShapeDtypeStruct((4, 4, 512)...  2.31 us

profile of v5, /device:TPU:1, one launch (start us, length us, event | category | flops | bytes accessed | tf_op | source)
XLA Modules:
  0.0 53.6 jit_solution(14201715610733097652)
XLA Ops:
  0.6 50.7 %shard_map.223 = (f32[32,512]{1,0:T(8,128)S(1)}, bf16[32,32,256]{2,1,0:T(8,128)(2,1)S(1)}, f32[128,128]{1,0:T(8,128)S(1)}, bf16[2,2048,256]{2,1,0:T(8,128)(2,1)S(1)}) custom-call(s32[4,4]{1,0:T(4,128)} %slot_hbm.1, bf16[32,32,256]{2,1,0:T(8,128)(2,1)} %feat_hbm.1, bf16[32,512]{1,0:T(8,128)(2,1)} %bitcast.12, f32[7,7,256]{2,1,0:T(8,128)} %cw_hbm.1, ...), custom_call_target="tpu_custom_call" | custom-call | flops 4000000000 | bytes 8000000 | tf_op jit(solution)/shard_map/pallas_call | solution.py:819
  51.3 2.3 %shard_map.224 = (bf16[4,4,512]{2,1,0:T(4,128)(2,1)}, bf16[32,32,256]{2,1,0:T(8,128)(2,1)}, f32[7,7,256]{2,1,0:T(8,128)}, f32[256,1024]{1,0:T(8,128)}, f32[1024,...) custom-call(f32[32,512]{1,0:T(8,128)S(1)} %get-tuple-element.22.pooled_in, ...), custom_call_target="tpu_custom_call" | custom-call | flops 1000000 | bytes 7000000 | tf_op jit(solution)/shard_map/pallas_call | solution.py:765
